TPU v7x, 256 devices: a whole 4x4x8 slice. The times are simulated.
256 devices in a mesh: dp: 32 (over x, z), tensor: 8 (over y, core).
Axes of the slice: x: 4, y: 4, z: 8, core: 2. Of those that a mesh axis runs over, the one named last changes fastest.
Arguments:
- queries: bfloat16 [3072, 3, 4096], P('dp', None, 'tensor'), may hold values from -600 to 600
- prompt_cache: bfloat16 [64, 2, 4096, 1024], P('dp', None, None, 'tensor'), may hold values from -6 to 6
- tails: bfloat16 [3072, 2, 64, 1024], P('dp', None, None, 'tensor'), may hold values from -5 to 5
- fresh: bfloat16 [3072, 3, 2, 1024], P('dp', None, None, 'tensor'), may hold values from -5 to 5
- residual: bfloat16 [3072, 3, 4096], P('dp', None, 'tensor'), may hold values from -6 to 6
- out_proj: bfloat16 [4096, 4096], P('tensor'), may hold values from -0.75 to 0.75
- lengths: int32 [3072], P('dp'), may hold values from 1 to 61, as said below
- prompt_of: int32 [3072], P('dp'), may hold values from 0 to 63, as said below
- moves: int32 [496, 3], replicated, may hold values from 0 to 3071, as said below
Outputs:
- mixed: bfloat16 [4064, 3, 4096], P('dp', None, 'tensor')
- tails_out: bfloat16 [4064, 2, 64, 1024], P('dp', None, None, 'tensor')
Inputs may be any that keep to these rules, and one draw needn't show every extreme that they name: `lengths`: on every dp index some branch has exactly 61. `prompt_of`: branch b's prompt is one of the 2 prompts held by the same dp index: from (b // 96) * 2 to that plus 2 - 1. `moves`: column 0 is a branch, column 1 the dp index that holds it, column 2 another dp index. Half of the dp indices send and the other half receive; every sender sends exactly 31 branches and every receiver receives exactly 31; every sender sends two branches to every receiver but one and one branch to that one; no branch is listed twice.
All inputs are finite; a program needn't handle non-finite values.
Results may differ from a plain program's by a relative error of at most 0.018.
Values may be sent and summed in bfloat16 or wider, within the bound.
A program may use at most 128 MiB of HBM per device.

v0:
```python
import math

import jax
import jax.numpy as jnp
from jax import lax
from jax.sharding import PartitionSpec as P

HEAD = 128


def attend(grouped, cache_here, local_prompt, tails_here, fresh_here, lengths_here):
    branches_here, new_count, kv_local, share, head_size = grouped.shape
    scale = 1.0 / math.sqrt(head_size)
    tail_rows = tails_here.shape[2]
    prompt_rows = cache_here.shape[2]
    prefix = None
    for prompt_index in range(cache_here.shape[0]):
        keys_here = cache_here[prompt_index, 0].reshape(prompt_rows, kv_local, head_size)
        scores = (
            jnp.einsum("bnkgd,tkd->bnkgt", grouped, keys_here, preferred_element_type=jnp.float32)
            * scale
        )
        chosen = (local_prompt == prompt_index)[:, None, None, None, None]
        prefix = scores if prefix is None else jnp.where(chosen, scores, prefix)
    tail_keys = tails_here[:, 0].reshape(branches_here, tail_rows, kv_local, head_size)
    tail_scores = (
        jnp.einsum("bnkgd,btkd->bnkgt", grouped, tail_keys, preferred_element_type=jnp.float32)
        * scale
    )
    fresh_keys = fresh_here[:, :, 0].reshape(branches_here, new_count, kv_local, head_size)
    fresh_scores = (
        jnp.einsum("bnkgd,bmkd->bnkgm", grouped, fresh_keys, preferred_element_type=jnp.float32)
        * scale
    )
    tail_visible = (jnp.arange(tail_rows, dtype=jnp.int32)[None, :] < lengths_here[:, None])[
        :, None, None, None, :
    ]
    fresh_visible = (
        jnp.arange(new_count, dtype=jnp.int32)[None, :]
        <= jnp.arange(new_count, dtype=jnp.int32)[:, None]
    )[None, :, None, None, :]
    row_max = jnp.max(prefix, axis=-1, keepdims=True)
    row_max = jnp.maximum(
        row_max, jnp.max(jnp.where(tail_visible, tail_scores, -jnp.inf), axis=-1, keepdims=True)
    )
    row_max = jnp.maximum(
        row_max, jnp.max(jnp.where(fresh_visible, fresh_scores, -jnp.inf), axis=-1, keepdims=True)
    )
    prefix_expo = jnp.exp(prefix - row_max)
    tail_expo = jnp.where(tail_visible, jnp.exp(tail_scores - row_max), 0.0)
    fresh_expo = jnp.where(fresh_visible, jnp.exp(fresh_scores - row_max), 0.0)
    denominator = jnp.sum(prefix_expo, -1) + jnp.sum(tail_expo, -1) + jnp.sum(fresh_expo, -1)
    prefix_weights = prefix_expo.astype(jnp.bfloat16)
    accumulated = None
    for prompt_index in range(cache_here.shape[0]):
        values_here = cache_here[prompt_index, 1].reshape(prompt_rows, kv_local, head_size)
        chosen = (local_prompt == prompt_index)[:, None, None, None, None]
        term = jnp.einsum(
            "bnkgt,tkd->bnkgd",
            jnp.where(chosen, prefix_weights, 0.0),
            values_here,
            preferred_element_type=jnp.float32,
        )
        accumulated = term if accumulated is None else accumulated + term
    tail_values = tails_here[:, 1].reshape(branches_here, tail_rows, kv_local, head_size)
    accumulated = accumulated + jnp.einsum(
        "bnkgt,btkd->bnkgd",
        tail_expo.astype(jnp.bfloat16),
        tail_values,
        preferred_element_type=jnp.float32,
    )
    fresh_values = fresh_here[:, :, 1].reshape(branches_here, new_count, kv_local, head_size)
    accumulated = accumulated + jnp.einsum(
        "bnkgm,bmkd->bnkgd",
        fresh_expo.astype(jnp.bfloat16),
        fresh_values,
        preferred_element_type=jnp.float32,
    )
    result = accumulated / denominator[..., None]
    return result.astype(jnp.bfloat16).reshape(branches_here, new_count, -1)


def write_fresh(tails_here, fresh_here, lengths_here):
    tail_rows = tails_here.shape[2]
    new_count = fresh_here.shape[1]
    position = lengths_here[:, None, None] + jnp.arange(new_count, dtype=jnp.int32)[None, :, None]
    landing = jnp.arange(tail_rows, dtype=jnp.int32)[None, None, :] == position
    placed = jnp.einsum(
        "bit,bicx->bctx",
        landing.astype(jnp.bfloat16),
        fresh_here,
        preferred_element_type=jnp.float32,
    ).astype(jnp.bfloat16)
    covered = jnp.any(landing, axis=1)
    return jnp.where(covered[:, None, :, None], placed, tails_here)


def routing(moves, self_index, branches_here, groups, incoming):
    branch_ids = moves[:, 0]
    source = moves[:, 1]
    target = moves[:, 2]
    entries = jnp.arange(moves.shape[0], dtype=jnp.int32)
    earlier = entries[None, :] < entries[:, None]
    same_target = target[None, :] == target[:, None]
    arrival = jnp.sum((earlier & same_target).astype(jnp.int32), axis=1)
    pair_rank = jnp.sum(
        (earlier & same_target & (source[None, :] == source[:, None])).astype(jnp.int32), axis=1
    )
    outgoing = source == self_index
    arriving = target == self_index
    local_slot = branch_ids - self_index * branches_here
    buffer_rows = groups * 2
    buffer_index = jnp.arange(buffer_rows, dtype=jnp.int32)
    send_at = (buffer_index[None, :] == (target * 2 + pair_rank)[:, None]) & outgoing[:, None]
    from_slot = jnp.arange(branches_here, dtype=jnp.int32)[None, :] == local_slot[:, None]
    pack_matrix = jnp.dot(send_at.astype(jnp.float32).T, from_slot.astype(jnp.float32)).astype(
        jnp.bfloat16
    )
    leaving = jnp.sum((from_slot & outgoing[:, None]).astype(jnp.int32), axis=0)
    staying = leaving == 0
    place_at = (jnp.arange(incoming, dtype=jnp.int32)[None, :] == arrival[:, None]) & arriving[
        :, None
    ]
    take_from = buffer_index[None, :] == (source * 2 + pair_rank)[:, None]
    place_matrix = jnp.dot(place_at.astype(jnp.float32).T, take_from.astype(jnp.float32)).astype(
        jnp.bfloat16
    )
    return (pack_matrix, staying, place_matrix)


def route_rows(matrix, rows):
    flat = rows.reshape(rows.shape[0], -1)
    moved = jnp.dot(matrix, flat, preferred_element_type=jnp.float32).astype(jnp.bfloat16)
    return moved.reshape((matrix.shape[0],) + rows.shape[1:])


def keep_rows(staying, rows):
    shape_mask = staying.reshape((staying.shape[0],) + (1,) * (rows.ndim - 1))
    return jnp.where(shape_mask, rows, jnp.zeros((), rows.dtype))


def on_device(queries, prompt_cache, tails, fresh, residual, out_proj, lengths, prompt_of, moves):
    groups = lax.axis_size("dp")
    self_index = lax.axis_index("dp")
    branches_here = queries.shape[0]
    new_count = queries.shape[1]
    kv_local = tails.shape[3] // HEAD
    share = queries.shape[2] // (kv_local * HEAD)
    incoming = groups - 1
    local_prompt = prompt_of - self_index * prompt_cache.shape[0]
    grouped = queries.reshape(branches_here, new_count, kv_local, share, HEAD)
    heads_out = attend(grouped, prompt_cache, local_prompt, tails, fresh, lengths)
    tails_written = write_fresh(tails, fresh, lengths)
    pack_matrix, staying, place_matrix = routing(moves, self_index, branches_here, groups, incoming)
    arrived_heads, arrived_residual, arrived_tails = (
        lax.all_to_all(
            route_rows(pack_matrix, heads_out), "dp", split_axis=0, concat_axis=0, tiled=True
        ),
        lax.all_to_all(
            route_rows(pack_matrix, residual), "dp", split_axis=0, concat_axis=0, tiled=True
        ),
        lax.all_to_all(
            route_rows(pack_matrix, tails_written), "dp", split_axis=0, concat_axis=0, tiled=True
        ),
    )
    heads_slots = jnp.concatenate(
        [keep_rows(staying, heads_out), route_rows(place_matrix, arrived_heads)], axis=0
    )
    residual_slots = jnp.concatenate(
        [keep_rows(staying, residual), route_rows(place_matrix, arrived_residual)], axis=0
    )
    slot_count = heads_slots.shape[0]
    terms = jnp.dot(
        heads_slots.reshape(slot_count * new_count, -1),
        out_proj,
        preferred_element_type=jnp.float32,
    ).reshape(slot_count, new_count, -1)
    summed = lax.psum_scatter(
        terms.astype(jnp.bfloat16), "tensor", scatter_dimension=2, tiled=True
    ).astype(jnp.float32)
    mixed = (residual_slots.astype(jnp.float32) + summed).astype(jnp.bfloat16)
    tails_out = jnp.concatenate(
        [keep_rows(staying, tails_written), route_rows(place_matrix, arrived_tails)], axis=0
    )
    return (mixed, tails_out)


def solution(mesh):
    in_specs = (
        P("dp", None, "tensor"),
        P("dp", None, None, "tensor"),
        P("dp", None, None, "tensor"),
        P("dp", None, None, "tensor"),
        P("dp", None, "tensor"),
        P("tensor", None),
        P("dp"),
        P("dp"),
        P(),
    )
    out_specs = (P("dp", None, "tensor"), P("dp", None, None, "tensor"))
    return jax.shard_map(
        on_device, mesh=mesh, in_specs=in_specs, out_specs=out_specs, check_vma=False
    )
```

profile of v0, /device:TPU:16, one launch (start us, length us, event | category | flops | bytes accessed | tf_op | source)
XLA Modules:
  0.0 184.5 jit_solution(14637010275870650527)
XLA Ops:
  7.2 1.0 reshape.244
  8.2 10.4 %fusion.61 = f32[4096,96,3,4]{0,1,3,2:T(8,128)} fusion(bf16[2,2,4096,128]{3,2,1,0:T(8,128)(2,1)} %param.10, bf16[96,3,512]{2,0,1:T(8,128)(2,1)} %param.9), kind=kOutput, calls=%fused_computation.53 | convolution fusion | flops 1207959552 | bytes 20217856 | tf_op jit(solution)/shard_map/bnkgd,tkd->bnkgt/dot_general | solution.py:20
  18.9 2.0 %select_reduce_fusion = (f32[96,3,4]{2,1,0:T(4,128)S(1)}, f32[96,3,1,4,3]{3,4,1,0,2:T(4,128)S(1)}) fusion(pred[3,3]{1,0:T(4,128)(4,1)S(1)} %iota_compare_fusion.9, bf16[96,3,4,128]{3,2,0,1:T(4,128)(2,1)S(1)} %reshape.244, bf16[96,3,1,128]{3,2,1,0:T(2,128)(2,1)S(1)} %get-tuple-element.7), kind=kOutput, calls=%fused_computation.68 | convolution fusion | flops 893952 | bytes 387081 | tf_op jit(solution)/shard_map/bnkgd,bmkd->bnkgm/dot_general | solution.py:32
  21.1 2.5 %select_reduce_fusion.1 = (f32[96,3,4]{2,1,0:T(4,128)S(1)}, f32[96,1,64,3,4]{2,4,3,0,1:T(4,128)S(1)}) fusion(pred[96,64]{1,0:T(8,128)(4,1)S(1)} %iota_compare_fusion.8, bf16[96,3,4,128]{3,2,0,1:T(4,128)(2,1)S(1)} %reshape.244, bf16[96,2,64,128]{3,2,1,0:T(8,128)(2,1)} %param.11), kind=kOutput, calls=%fused_computation.69 | convolution fusion | flops 19094400 | bytes 2173440 | tf_op jit(solution)/shard_map/bnkgd,btkd->bnkgt/dot_general | solution.py:27
  23.7 12.4 %bitcast_reduce_fusion = (f32[96,3,4]{0,2,1:T(4,128)S(1)}, f32[1,4096,96,3,4]{1,2,4,3,0:T(8,128)}) fusion(bf16[2,2,4096,128]{3,2,1,0:T(8,128)(2,1)} %param.10, f32[4096,96,3,4]{0,1,3,2:T(8,128)} %fusion.61, pred[96]{0:T(512)(128)(4,1)S(1)} %get-tuple-element.16, bf16[96,3,512]{2,0,1:T(8,128)(2,1)S(1)} %copy-done), kind=kOutput, calls=%fused_computation.1 | convolution fusion | flops 1226832768 | bytes 39096928 | tf_op jit(solution)/shard_map/bnkgd,tkd->bnkgt/dot_general | solution.py:20
  36.3 9.0 %fusion.1 = f32[96,3,4]{0,2,1:T(4,128)S(1)} fusion(f32[1,4096,96,3,4]{1,2,4,3,0:T(8,128)} %get-tuple-element.20, f32[96,3,4]{0,2,1:T(4,128)S(1)} %maximum_maximum_fusion), kind=kLoop, calls=%fused_computation.6 | loop fusion | flops 9436032 | bytes 18883584 | tf_op jit(solution)/shard_map/reduce_sum | solution.py:52
  45.3 8.3 %fusion.3 = f32[96,3,4,128]{3,0,2,1:T(8,128)S(1)} fusion(pred[96]{0:T(512)(128)(4,1)S(1)} %get-tuple-element.16, f32[1,4096,96,3,4]{1,2,4,3,0:T(8,128)} %get-tuple-element.20, f32[96,3,4]{0,2,1:T(4,128)S(1)} %maximum_maximum_fusion, bf16[2,2,4096,128]{3,2,1,0:T(8,128)(2,1)} %param.10), kind=kOutput, calls=%fused_computation.8 | convolution fusion | flops 1222115328 | bytes 20517472 | tf_op jit(solution)/shard_map/bnkgt,tkd->bnkgd/dot_general | solution.py:58
  53.6 0.9 bitcast_reduce_fusion.1
  56.7 8.3 %fusion.55 = bf16[96,3,1,4,128]{4,0,3,1,2:T(8,128)(2,1)S(1)} fusion(f32[96,3,4,128]{3,0,2,1:T(8,128)S(1)} %fusion.3, pred[96]{0:T(512)(128)(4,1)S(1)} %get-tuple-element.15, f32[96,3,4]{0,2,1:T(4,128)S(1)} %maximum_maximum_fusion, f32[1,4096,96,3,4]{1,2,4,3,0:T(8,128)} %get-tuple-element.20, bf16[2,2,4096,128]{3,2,1,0:T(8,128)(2,1)} %param.10, ...), kind=kOutput, calls=%fused_computation.51 | convolution fusion | flops 1222852608 | bytes 21996640 | tf_op jit(solution)/shard_map/bnkgt,tkd->bnkgd/dot_general | solution.py:58
  66.4 0.8 reshape.257
  67.2 11.3 %all-to-all-start.1 = ((bf16[64,3,512]{2,1,0:T(4,128)(2,1)}), bf16[64,3,512]{2,1,0:T(4,128)(2,1)S(1)}, u32[]{:S(2)}, u32[]{:S(2)}) async-start(bf16[64,3,512]{2,1,0:T(4,128)(2,1)} %reshape.257), calls=%async_computation.1 | async-start | bytes 524288 | tf_op jit(solution)/shard_map/all_to_all | solution.py:156
  79.8 11.2 %all-to-all-done.1 = bf16[64,3,512]{2,1,0:T(4,128)(2,1)S(1)} async-done(((bf16[64,3,512]{2,1,0:T(4,128)(2,1)}), bf16[64,3,512]{2,1,0:T(4,128)(2,1)S(1)}, u32[]{:S(2)}, u32[]{:S(2)}) %all-to-all-start.1) | async-done | bytes 196640 | tf_op jit(solution)/shard_map/all_to_all | solution.py:156
  91.3 5.7 %convolution_convert_fusion.2 = bf16[127,3,4096]{2,0,1:T(8,128)(2,1)} fusion(bf16[512,4096]{1,0:T(8,128)(2,1)} %param.14, bf16[31,3,512]{2,0,1:T(8,128)(2,1)S(1)} %copy.109, bf16[96,3,512]{2,0,1:T(8,128)(2,1)S(1)} %get-tuple-element.14), kind=kOutput, calls=%fused_computation.16 | convolution fusion | flops 1600370688 | bytes 7705600 | tf_op jit(solution)/shard_map/dot_general | solution.py:173
  97.3 0.8 reshape.240
  98.1 4.4 %all-to-all-start = ((bf16[64,3,512]{2,1,0:T(4,128)(2,1)}), bf16[64,3,512]{2,1,0:T(4,128)(2,1)S(1)}, u32[]{:S(2)}, u32[]{:S(2)}) async-start(bf16[64,3,512]{2,1,0:T(4,128)(2,1)} %reshape.240), calls=%async_computation | async-start | bytes 524288 | tf_op jit(solution)/shard_map/all_to_all | solution.py:159
  102.8 5.6 %broadcast_select_fusion = (bf16[96,2,64,128]{3,2,1,0:T(8,128)(2,1)}, bf16[96,2,64,128]{3,2,1,0:T(8,128)(2,1)S(1)}) fusion(pred[96]{0:T(512)(128)(4,1)S(1)} %broadcast_compare_fusion, bf16[96,2,64,128]{3,2,1,0:T(8,128)(2,1)} %param.11, bf16[96,3,2,128]{3,2,1,0:T(2,128)(2,1)S(1)} %copy-done.3, s32[96,3]{1,0:T(8,128)S(1)} %iota_add_fusion, ...), kind=kOutput, calls=%fused_computation.24 | convolution fusion | flops 14174208 | bytes 9592032 | tf_op jit(solution)/shard_map/bit,bicx->bctx/dot_general | solution.py:88
  108.4 2.3 %fusion.20 = bf16[8,8,128,128]{3,1,2,0:T(8,128)(2,1)S(1)} fusion(bf16[64,96]{1,0:T(8,128)(2,1)S(1)} %convolution_convert_fusion.7, bf16[12,8,128,128]{3,2,1,0:T(8,128)(2,1)S(1)} %bitcast.241), kind=kOutput, calls=%fused_computation.31 | convolution fusion | flops 202375168 | bytes 5255168 | tf_op jit(solution)/shard_map/dot_general | solution.py:133
  110.7 2.0 %copy.130 = bf16[8,8,128,128]{3,2,1,0:T(8,128)(2,1)} copy(bf16[8,8,128,128]{3,1,2,0:T(8,128)(2,1)S(1)} %fusion.20) | data formatting | bytes 4194304
  112.7 1.3 all-to-all-done
  113.9 8.5 %all-to-all-start.2 = ((bf16[64,2,64,128]{3,2,1,0:T(8,128)(2,1)}), bf16[64,2,64,128]{3,2,1,0:T(8,128)(2,1)S(1)}, u32[]{:S(2)}, u32[]{:S(2)}) async-start(bf16[64,2,64,128]{3,2,1,0:T(8,128)(2,1)} %bitcast.94), calls=%async_computation.3 | async-start | bytes 4194304 | tf_op jit(solution)/shard_map/all_to_all | solution.py:162
  122.8 48.7 %all-to-all-done.2 = bf16[64,2,64,128]{3,2,1,0:T(8,128)(2,1)S(1)} async-done(((bf16[64,2,64,128]{3,2,1,0:T(8,128)(2,1)}), bf16[64,2,64,128]{3,2,1,0:T(8,128)(2,1)S(1)}, u32[]{:S(2)}, u32[]{:S(2)}) %all-to-all-start.2) | async-done | bytes 2097184 | tf_op jit(solution)/shard_map/all_to_all | solution.py:162
  171.5 1.5 convolution_convert_fusion.1
  173.4 2.4 %pad_maximum_fusion = bf16[127,2,64,128]{3,2,1,0:T(8,128)(2,1)} fusion(bf16[31,2,64,128]{3,2,1,0:T(8,128)(2,1)S(1)} %bitcast.240, bf16[96,2,64,128]{3,2,1,0:T(8,128)(2,1)S(1)} %copy-done.1), kind=kLoop, calls=%fused_computation.20 | loop fusion | flops 2080768 | bytes 8323072 | tf_op jit(solution)/shard_map/concatenate | solution.py:182
  175.8 1.9 %add_convert_fusion = bf16[127,3,512]{2,0,1:T(8,128)(2,1)} fusion(bf16[127,3,512]{2,0,1:T(8,128)(2,1)} %reduce-scatter.2.cloned.1.call-done, bf16[31,3,512]{2,0,1:T(8,128)(2,1)S(1)} %copy.89, bf16[96,3,512]{2,0,1:T(8,128)(2,1)S(1)} %get-tuple-element.13), kind=kLoop, calls=%fused_computation.63 | loop fusion | flops 1365504 | bytes 1170432 | tf_op jit(solution)/shard_map/convert_element_type | solution.py:181
  (61 shorter events, 6.9 us)
Async XLA Ops:
  8.2 10.4 %copy-start.3 = (bf16[96,3,2,128]{3,2,1,0:T(2,128)(2,1)S(1)}, bf16[96,3,2,128]{3,2,1,0:T(2,128)(2,1)}, u32[]{:S(2)}) copy-start(bf16[96,3,2,128]{3,2,1,0:T(2,128)(2,1)} %param.12) | copy-start | bytes 442372
  8.2 12.8 %copy-start.5 = (s32[96]{0:T(128)S(1)}, s32[96]{0:T(128)}, u32[]{:S(2)}) copy-start(s32[96]{0:T(128)} %param.15) | copy-start | bytes 1156
  18.7 5.0 %copy-start.6 = (s32[96]{0:T(128)S(1)}, s32[96]{0:T(128)}, u32[]{:S(2)}) copy-start(s32[96]{0:T(128)} %param.16) | copy-start | bytes 1156
  18.7 5.1 %copy-start = (bf16[96,3,512]{2,0,1:T(8,128)(2,1)S(1)}, bf16[96,3,512]{2,0,1:T(8,128)(2,1)}, u32[]{:S(2)}) copy-start(bf16[96,3,512]{2,0,1:T(8,128)(2,1)} %param.9) | copy-start | bytes 884740
  45.3 9.2 %copy-start.7 = (bf16[96,2,64,128]{3,2,1,0:T(8,128)(2,1)S(1)}, bf16[96,2,64,128]{3,2,1,0:T(8,128)(2,1)}, u32[]{:S(2)}) copy-start(bf16[96,2,64,128]{3,2,1,0:T(8,128)(2,1)} %param.11) | copy-start | bytes 9437188
  53.6 1.6 copy-start.4
  65.0 14.7 %copy-start.2 = (bf16[96,3,512]{2,0,1:T(8,128)(2,1)S(1)}, bf16[96,3,512]{2,0,1:T(8,128)(2,1)}, u32[]{:S(2)}) copy-start(bf16[96,3,512]{2,0,1:T(8,128)(2,1)} %param.13) | copy-start | bytes 884740
  67.2 23.8 %all-to-all-start.1 = ((bf16[64,3,512]{2,1,0:T(4,128)(2,1)}), bf16[64,3,512]{2,1,0:T(4,128)(2,1)S(1)}, u32[]{:S(2)}, u32[]{:S(2)}) async-start(bf16[64,3,512]{2,1,0:T(4,128)(2,1)} %reshape.257), calls=%async_computation.1 | async-start | bytes 524288 | tf_op jit(solution)/shard_map/all_to_all | solution.py:156
  78.5 97.3 %reduce-scatter.2.cloned.1.call-start = ((), (), s32[]{:S(2)}) async-start(), calls=%async_computation.4 | async-start | bytes 3538944 | tf_op jit(solution)/shard_map/reduce_scatter | solution.py:178
  98.1 15.8 %all-to-all-start = ((bf16[64,3,512]{2,1,0:T(4,128)(2,1)}), bf16[64,3,512]{2,1,0:T(4,128)(2,1)S(1)}, u32[]{:S(2)}, u32[]{:S(2)}) async-start(bf16[64,3,512]{2,1,0:T(4,128)(2,1)} %reshape.240), calls=%async_computation | async-start | bytes 524288 | tf_op jit(solution)/shard_map/all_to_all | solution.py:159
  113.9 57.6 %all-to-all-start.2 = ((bf16[64,2,64,128]{3,2,1,0:T(8,128)(2,1)}), bf16[64,2,64,128]{3,2,1,0:T(8,128)(2,1)S(1)}, u32[]{:S(2)}, u32[]{:S(2)}) async-start(bf16[64,2,64,128]{3,2,1,0:T(8,128)(2,1)} %bitcast.94), calls=%async_computation.3 | async-start | bytes 4194304 | tf_op jit(solution)/shard_map/all_to_all | solution.py:162
  171.5 1.9 %copy-start.1 = (bf16[96,2,64,128]{3,2,1,0:T(8,128)(2,1)S(1)}, bf16[96,2,64,128]{3,2,1,0:T(8,128)(2,1)}, u32[]{:S(2)}) copy-start(bf16[96,2,64,128]{3,2,1,0:T(8,128)(2,1)} %get-tuple-element.23) | copy-start | bytes 9437188
Sparse Core Ops, SparseCore 0:
  97.2 29.2 reduce-scatter.1
where the time goes:
time: 185 us
  matrix products  61.9 us (33%)
  waiting for transfers between devices  61.2 us (33%)
  starting transfers between devices  24.5 us (13%)
  other arithmetic  15.9 us (9%)
  between operations  14.4 us (8%)
  local copies, waits for them, and re-layouts  6.66 us (4%)
    all_to_all x1, waiting for transfers between devices, on_device(): lax.all_to_all(route_rows(pack_matrix, tails_written), 'dp', split_axis=0...  48.7 us
    dot_general x2, matrix products, attend(): jnp.einsum('bnkgd,tkd->bnkgt', grouped, keys_here, preferred_element_type...  22.8 us
    dot_general x2, matrix products, attend(): jnp.einsum('bnkgt,tkd->bnkgd', jnp.where(chosen, prefix_weights, 0.0), va...  16.6 us
    all_to_all x1, starting transfers between devices, on_device(): lax.all_to_all(route_rows(pack_matrix, heads_out), 'dp', split_axis=0, co...  11.3 us
    all_to_all x1, waiting for transfers between devices, on_device(): lax.all_to_all(route_rows(pack_matrix, heads_out), 'dp', split_axis=0, co...  11.2 us
    reduce_sum x1, other arithmetic, attend(): jnp.sum(prefix_expo, -1) + jnp.sum(tail_expo, -1) + jnp.sum(fresh_expo, -1)  8.98 us
    all_to_all x1, starting transfers between devices, on_device(): lax.all_to_all(route_rows(pack_matrix, tails_written), 'dp', split_axis=0...  8.53 us
    dot_general x1, matrix products, on_device(): jnp.dot(heads_slots.reshape(slot_count * new_count, -1), out_proj, prefer...  5.72 us
  transfers between devices with their start and end apart: 4, of which 3 were waited for; matrix products, arithmetic and copies ran while one was open for 9% of the time, Pallas kernels for 0%

commit v1 on v0

v1 whole, which is shorter than its diff:
```python
import math

import jax
import jax.numpy as jnp
from jax import lax
from jax.experimental import pallas as pl
from jax.experimental.pallas import tpu as pltpu
from jax.sharding import PartitionSpec as P

HEAD = 128
GROUP = 16
TILES = 2
CHUNK = 512
CORES = 2
ROW = 16
MIB = 1 << 20
MESH = pl.DeviceIdType.MESH


def written_rows(rows, fresh, length):
    at = lax.broadcasted_iota(jnp.int32, rows.shape, 0)
    wide = rows.astype(jnp.float32)
    for i, line in enumerate(fresh):
        wide = jnp.where(at == length + i, line, wide)
    return wide.astype(rows.dtype)


def fresh_of(fresh_ref, branch, kind):
    pairs = [fresh_ref[branch, i].astype(jnp.float32) for i in range(fresh_ref.shape[1])]
    return [pair[kind : kind + 1] for pair in pairs]


def attend_tile(first, query_ref, cache, tails, fresh_wide, length_ref, second_ref, heads, scores):
    new_count = query_ref.shape[0]
    share = query_ref.shape[2] // HEAD
    keys = cache.shape[2]
    tail_rows = tails.shape[2]
    tail_keys = GROUP * tail_rows
    blocks = new_count * share
    rows = blocks * GROUP
    factor = math.log2(math.e) / math.sqrt(HEAD)
    contract_last = (((1,), (1,)), ((), ()))

    def lanes(op, value, carry):
        for at in range(0, value.shape[1], HEAD):
            carry = op(carry, value[:, at : at + HEAD])
        return carry

    def fresh_block(kind):
        parts = [fresh_wide[kind, i, pl.ds(first, GROUP)] for i in range(new_count)]
        parts.append(jnp.zeros((HEAD - new_count * GROUP, HEAD), jnp.float32))
        return jnp.concatenate(parts, axis=0).astype(jnp.bfloat16)

    query = jnp.concatenate(
        [
            query_ref[i, pl.ds(first, GROUP), h * HEAD : (h + 1) * HEAD]
            for i in range(new_count)
            for h in range(share)
        ],
        axis=0,
    )
    second = jnp.concatenate([second_ref[pl.ds(first, GROUP)]] * blocks, axis=0) > 0
    nothing = jnp.zeros_like(query)
    both = jnp.concatenate(
        [jnp.where(second, nothing, query), jnp.where(second, query, nothing)], axis=1
    )
    top = jnp.full((rows, HEAD), -jnp.inf, jnp.float32)
    for at in range(0, keys, CHUNK):
        key_block = jnp.concatenate(
            [cache[0, 0, at : at + CHUNK], cache[1, 0, at : at + CHUNK]], axis=1
        )
        block = lax.dot_general(both, key_block, contract_last, preferred_element_type=jnp.float32)
        scores[:, at : at + CHUNK] = block
        top = lanes(jnp.maximum, block, top)
    tail_scores = lax.dot_general(
        query,
        tails[pl.ds(first, GROUP), 0].reshape(tail_keys, HEAD),
        contract_last,
        preferred_element_type=jnp.float32,
    )
    length = jnp.concatenate([length_ref[pl.ds(first, GROUP)]] * blocks, axis=0)
    row_at = lax.broadcasted_iota(jnp.int32, (rows, HEAD), 0)
    key_at = lax.broadcasted_iota(jnp.int32, (rows, HEAD), 1)
    held = []
    for at in range(0, tail_keys, HEAD):
        seen = (row_at % GROUP == (key_at + at) // tail_rows) & (key_at % tail_rows < length)
        held.append(jnp.where(seen, tail_scores[:, at : at + HEAD], -jnp.inf))
    tail_scores = jnp.concatenate(held, axis=1)
    fresh_scores = lax.dot_general(
        query, fresh_block(0), contract_last, preferred_element_type=jnp.float32
    )
    seen = (row_at % GROUP == key_at % GROUP) & (key_at // GROUP <= row_at // (GROUP * share))
    fresh_scores = jnp.where(seen, fresh_scores, -jnp.inf)
    top = jnp.maximum(lanes(jnp.maximum, tail_scores, top), fresh_scores)
    top = jnp.max(top, axis=1, keepdims=True)
    total = jnp.zeros((rows, HEAD), jnp.float32)
    pair = jnp.zeros((rows, 2 * HEAD), jnp.float32)
    for at in range(0, keys, CHUNK):
        expo = jnp.exp2((scores[:, at : at + CHUNK] - top) * factor)
        total = lanes(jnp.add, expo, total)
        value_block = jnp.concatenate(
            [cache[0, 1, at : at + CHUNK], cache[1, 1, at : at + CHUNK]], axis=1
        )
        pair += jnp.dot(expo.astype(jnp.bfloat16), value_block, preferred_element_type=jnp.float32)
    mixed = jnp.where(second, pair[:, HEAD:], pair[:, :HEAD])
    expo = jnp.exp2((tail_scores - top) * factor)
    total = lanes(jnp.add, expo, total)
    mixed += jnp.dot(
        expo.astype(jnp.bfloat16),
        tails[pl.ds(first, GROUP), 1].reshape(tail_keys, HEAD),
        preferred_element_type=jnp.float32,
    )
    expo = jnp.exp2((fresh_scores - top) * factor)
    total += expo
    mixed += jnp.dot(
        expo.astype(jnp.bfloat16), fresh_block(1), preferred_element_type=jnp.float32
    )
    result = (mixed / jnp.sum(total, axis=1, keepdims=True)).astype(heads.dtype)
    for i in range(new_count):
        for h in range(share):
            at = (i * share + h) * GROUP
            heads[i, pl.ds(first, GROUP), h * HEAD : (h + 1) * HEAD] = result[at : at + GROUP]


def block_kernel(
    groups,
    chips,
    take_ref,
    branch_length_ref,
    stay_ref,
    query_ref,
    residual_ref,
    fresh_ref,
    length_ref,
    second_ref,
    tails_in,
    cache_in,
    proj_in,
    rows_out,
    arrived_rows,
    arrived_tails,
    home_out,
    tails,
    cache,
    proj,
    staged,
    staged_rows,
    fresh_wide,
    scores,
    heads,
    own,
    pair_send,
    pair_recv,
    chip_send,
    chip_recv,
    wide_rows,
    load_sems,
    tail_send_sems,
    tail_recv_sems,
    row_send_sems,
    row_recv_sems,
    pair_send_sems,
    pair_recv_sems,
    chip_send_sems,
    chip_recv_sems,
):
    new_count, branches_here, width = query_ref.shape
    me = lax.axis_index("dp")
    place = lax.axis_index("tensor")
    chip, core = place // CORES, place % CORES
    other = chip * CORES + (CORES - 1 - core)
    spans = GROUP * TILES
    chunks = branches_here // spans

    def peer_of(step):
        return lax.rem(me + step, groups)

    def chip_of(step):
        return lax.rem(chip + step, chips)

    barrier = pltpu.get_barrier_semaphore()

    def greet(step, carry):
        pl.semaphore_signal(
            barrier, inc=1, device_id=(peer_of(step), place), device_id_type=MESH
        )
        return carry

    load_tails = pltpu.make_async_copy(tails_in, tails, load_sems.at[0])
    load_cache = pltpu.make_async_copy(cache_in, cache, load_sems.at[1])
    load_proj = pltpu.make_async_copy(proj_in, proj, load_sems.at[2])
    load_tails.start()
    load_cache.start()
    load_proj.start()
    lax.fori_loop(1, groups, greet, 0)
    pl.semaphore_signal(barrier, inc=1, device_id=(me, other), device_id_type=MESH)
    for step in range(1, chips):
        pl.semaphore_signal(
            barrier,
            inc=1,
            device_id=(me, chip_of(step) * CORES + core),
            device_id_type=MESH,
        )

    load_tails.wait()

    def pack(slot, carry):
        branch = take_ref[slot]
        length = branch_length_ref[branch]
        for kind in range(2):
            staged[slot // 2, slot % 2, kind] = written_rows(
                tails[branch, kind], fresh_of(fresh_ref, branch, kind), length
            )
        return carry

    lax.fori_loop(0, groups * 2, pack, 0)
    pl.semaphore_wait(barrier, groups - 1 + 1 + chips - 1)

    def tail_copy(step):
        return pltpu.make_async_remote_copy(
            src_ref=staged.at[peer_of(step)],
            dst_ref=arrived_tails.at[me],
            send_sem=tail_send_sems.at[step],
            recv_sem=tail_recv_sems.at[step],
            device_id=(peer_of(step), place),
            device_id_type=MESH,
        )

    def row_copy(step):
        return pltpu.make_async_remote_copy(
            src_ref=staged_rows.at[peer_of(step)],
            dst_ref=arrived_rows.at[me],
            send_sem=row_send_sems.at[step],
            recv_sem=row_recv_sems.at[step],
            device_id=(peer_of(step), place),
            device_id_type=MESH,
        )

    def pair_copy(chunk):
        return pltpu.make_async_remote_copy(
            src_ref=pair_send.at[chunk],
            dst_ref=pair_recv.at[chunk],
            send_sem=pair_send_sems.at[chunk],
            recv_sem=pair_recv_sems.at[chunk],
            device_id=(me, other),
            device_id_type=MESH,
        )

    def chip_copy(chunk, step):
        return pltpu.make_async_remote_copy(
            src_ref=chip_send.at[chunk, step - 1],
            dst_ref=chip_recv.at[chunk, step - 1],
            send_sem=chip_send_sems.at[chunk, step - 1],
            recv_sem=chip_recv_sems.at[chunk, step - 1],
            device_id=(me, chip_of(step) * CORES + core),
            device_id_type=MESH,
        )

    def send_tails(step, carry):
        tail_copy(step).start()
        return carry

    lax.fori_loop(1, groups, send_tails, 0)

    def widen(branch, carry):
        for i in range(new_count):
            both = fresh_ref[branch, i].astype(jnp.float32)
            for kind in range(2):
                fresh_wide[kind, i, pl.ds(branch, 1)] = both[kind : kind + 1]
        return carry

    lax.fori_loop(0, branches_here, widen, 0)
    load_cache.wait()
    load_proj.wait()

    def project(chunk):
        first = pl.multiple_of(chunk * spans, spans)
        lhs = jnp.concatenate([heads[i, pl.ds(first, spans)] for i in range(new_count)], axis=0)
        for y in range(chips):
            column = pl.multiple_of((y * CORES + core) * width, width)
            own[chunk, y] = jnp.dot(
                lhs, proj[:, pl.ds(column, width)], preferred_element_type=jnp.float32
            )
            column = pl.multiple_of((y * CORES + CORES - 1 - core) * width, width)
            pair_send[chunk, y] = jnp.dot(
                lhs, proj[:, pl.ds(column, width)], preferred_element_type=jnp.float32
            ).astype(pair_send.dtype)
        pair_copy(chunk).start()

    def exchange(chunk):
        pair_copy(chunk).wait()
        for step in range(1, chips):
            y = chip_of(step)
            both = own[chunk, y] + pair_recv[chunk, y].astype(jnp.float32)
            chip_send[chunk, step - 1] = both.astype(chip_send.dtype)
            chip_copy(chunk, step).start()

    def finish(chunk):
        first = pl.multiple_of(chunk * spans, spans)
        summed = own[chunk, chip] + pair_recv[chunk, chip].astype(jnp.float32)
        for step in range(1, chips):
            chip_copy(chunk, step).wait()
            summed += chip_recv[chunk, step - 1].astype(jnp.float32)
        for i in range(new_count):
            rows = summed[i * spans : (i + 1) * spans]
            rows += residual_ref[i, pl.ds(first, spans)].astype(jnp.float32)
            rows_out[i, pl.ds(first, spans)] = rows.astype(rows_out.dtype)
            for at in range(0, width, HEAD):
                wide_rows[pl.ds(first, spans), i * (width // HEAD) + at // HEAD] = rows[
                    :, at : at + HEAD
                ]

    def work(chunk, carry):
        def tile(index, inner):
            first = pl.multiple_of((chunk * TILES + index) * GROUP, GROUP)
            attend_tile(
                first, query_ref, cache, tails, fresh_wide, length_ref, second_ref, heads, scores
            )
            return inner

        lax.fori_loop(0, TILES, tile, 0)

        @pl.when(chunk > 0)
        def _():
            exchange(chunk - 1)

        project(chunk)
        return carry

    lax.fori_loop(0, chunks, work, 0)
    exchange(chunks - 1)

    def settle(branch, carry):
        keep = stay_ref[branch] > 0
        length = branch_length_ref[branch]
        for kind in range(2):
            rows = written_rows(tails[branch, kind], fresh_of(fresh_ref, branch, kind), length)
            tails[branch, kind] = jnp.where(keep, rows, jnp.zeros_like(rows))
        return carry

    def finish_chunk(chunk, carry):
        finish(chunk)
        return carry

    wide_rows[...] = jnp.zeros_like(wide_rows)
    lax.fori_loop(0, chunks, finish_chunk, 0)

    def pack_rows(slot, carry):
        staged_rows[slot // 2, slot % 2] = wide_rows[take_ref[slot]].astype(staged_rows.dtype)
        return carry

    lax.fori_loop(0, groups * 2, pack_rows, 0)

    def send_rows(step, carry):
        row_copy(step).start()
        return carry

    lax.fori_loop(1, groups, send_rows, 0)
    lax.fori_loop(0, branches_here, settle, 0)
    store_home = pltpu.make_async_copy(tails, home_out, load_sems.at[3])
    store_home.start()
    store_home.wait()

    def drain(step, carry):
        row_copy(step).wait()
        tail_copy(step).wait()
        return carry

    lax.fori_loop(1, groups, drain, 0)


def block(take, stay, lengths, queries, residual, fresh, length_rows, second, tails, cache, proj):
    groups, chips = lax.axis_size("dp"), lax.axis_size("tensor") // CORES
    new_count, branches_here, width = queries.shape
    spans = GROUP * TILES
    chunks = branches_here // spans
    rows = new_count * (width // HEAD) * GROUP
    kind = queries.dtype
    smem = pl.BlockSpec(memory_space=pltpu.SMEM)
    vmem = pl.BlockSpec(memory_space=pltpu.VMEM)
    hbm = pl.BlockSpec(memory_space=pl.ANY)
    flops = 8 * new_count * branches_here * (width // HEAD) * cache.shape[2] * HEAD
    dma = pltpu.SemaphoreType.DMA

    def body(*refs):
        block_kernel(groups, chips, *refs)

    return pl.pallas_call(
        body,
        out_shape=[
            jax.ShapeDtypeStruct(queries.shape, kind),
            jax.ShapeDtypeStruct((groups, 2, ROW, HEAD), kind),
            jax.ShapeDtypeStruct((groups, 2) + tails.shape[1:], kind),
            jax.ShapeDtypeStruct(tails.shape, kind),
        ],
        in_specs=[smem] * 3 + [vmem] * 5 + [hbm] * 3,
        out_specs=[vmem, hbm, hbm, hbm],
        scratch_shapes=[
            pltpu.VMEM(tails.shape, kind),
            pltpu.VMEM(cache.shape, kind),
            pltpu.VMEM(proj.shape, kind),
            pltpu.VMEM((groups, 2) + tails.shape[1:], kind),
            pltpu.VMEM((groups, 2, ROW, HEAD), kind),
            pltpu.VMEM((2, new_count, branches_here, HEAD), jnp.float32),
            pltpu.VMEM((rows, cache.shape[2]), jnp.float32),
            pltpu.VMEM(queries.shape, kind),
            pltpu.VMEM((chunks, chips, new_count * spans, width), jnp.float32),
            pltpu.VMEM((chunks, chips, new_count * spans, width), kind),
            pltpu.VMEM((chunks, chips, new_count * spans, width), kind),
            pltpu.VMEM((chunks, chips - 1, new_count * spans, width), kind),
            pltpu.VMEM((chunks, chips - 1, new_count * spans, width), kind),
            pltpu.VMEM((branches_here, ROW, HEAD), jnp.float32),
            dma((4,)),
            dma((groups,)),
            dma((groups,)),
            dma((groups,)),
            dma((groups,)),
            dma((chunks,)),
            dma((chunks,)),
            dma((chunks, chips - 1)),
            dma((chunks, chips - 1)),
        ],
        cost_estimate=pl.CostEstimate(
            flops=flops, bytes_accessed=20 * MIB, transcendentals=flops // 1024
        ),
        compiler_params=pltpu.CompilerParams(
            collective_id=0, has_side_effects=True, vmem_limit_bytes=52 * MIB
        ),
    )(take, lengths, stay, queries, residual, fresh, length_rows, second, tails, cache, proj)


def place_kernel(
    take_ref,
    keep_ref,
    rows_ref,
    arrived_rows_ref,
    home_ref,
    arrived_ref,
    mixed_ref,
    out_ref,
    blank,
    stage,
    sems,
    home_sem,
):
    incoming = take_ref.shape[0]
    new_count, first, width = rows_ref.shape
    lines = new_count * (width // HEAD)
    copy_home = pltpu.make_async_copy(home_ref, out_ref.at[pl.ds(0, first)], home_sem)
    copy_home.start()
    blank[...] = jnp.zeros_like(blank)

    def start(row, carry):
        source = take_ref[row]

        @pl.when(source >= 0)
        def _():
            pltpu.make_async_copy(
                arrived_ref.at[source], out_ref.at[first + row], sems.at[row]
            ).start()

        @pl.when(source < 0)
        def _():
            pltpu.make_async_copy(blank, out_ref.at[first + row], sems.at[row]).start()

        return carry

    def stage_row(row, carry):
        source = take_ref[row]
        value = arrived_rows_ref[jnp.maximum(source, 0)].astype(jnp.float32)
        value = jnp.where(source >= 0, value, 0.0)
        for line in range(lines):
            stage[line, pl.ds(row, 1)] = value[line : line + 1]
        return carry

    def done(row, carry):
        pltpu.make_async_copy(blank, out_ref.at[first + row], sems.at[row]).wait()
        return carry

    lax.fori_loop(0, incoming, start, 0)
    lax.fori_loop(0, incoming, stage_row, 0)
    keep = jnp.concatenate([keep_ref[...]] * (width // HEAD), axis=1) > 0
    for i in range(new_count):
        rows = rows_ref[i]
        mixed_ref[i, :first] = jnp.where(keep, rows, jnp.zeros_like(rows))
        for at in range(0, width, HEAD):
            line = i * (width // HEAD) + at // HEAD
            mixed_ref[i, first:, at : at + HEAD] = stage[line, :incoming].astype(mixed_ref.dtype)
    lax.fori_loop(0, incoming, done, 0)
    copy_home.wait()


def place(take, keep, rows, arrived_rows, home, arrived):
    incoming = take.shape[0]
    new_count, branches_here, width = rows.shape
    slots = branches_here + incoming
    smem = pl.BlockSpec(memory_space=pltpu.SMEM)
    vmem = pl.BlockSpec(memory_space=pltpu.VMEM)
    hbm = pl.BlockSpec(memory_space=pl.ANY)
    return pl.pallas_call(
        place_kernel,
        out_shape=[
            jax.ShapeDtypeStruct((new_count, slots, width), rows.dtype),
            jax.ShapeDtypeStruct((slots,) + home.shape[1:], home.dtype),
        ],
        in_specs=[smem, vmem, vmem, vmem, hbm, hbm],
        out_specs=[vmem, hbm],
        scratch_shapes=[
            pltpu.VMEM(home.shape[1:], home.dtype),
            pltpu.VMEM((new_count * (width // HEAD), incoming + 1, HEAD), jnp.float32),
            pltpu.SemaphoreType.DMA((incoming,)),
            pltpu.SemaphoreType.DMA(()),
        ],
        compiler_params=pltpu.CompilerParams(vmem_limit_bytes=8 * MIB),
    )(take, keep, rows, arrived_rows, home, arrived)


def routing(moves, self_index, branches_here, groups, incoming):
    branch_ids, source, target = moves[:, 0], moves[:, 1], moves[:, 2]
    entries = jnp.arange(moves.shape[0], dtype=jnp.int32)
    earlier = entries[None, :] < entries[:, None]
    same_target = earlier & (target[None, :] == target[:, None])
    arrival = jnp.sum(same_target.astype(jnp.int32), axis=1)
    rank = jnp.sum((same_target & (source[None, :] == source[:, None])).astype(jnp.int32), axis=1)
    local_slot = branch_ids - self_index * branches_here
    slots = jnp.arange(groups * 2, dtype=jnp.int32)
    sent = (source == self_index)[None, :] & ((target * 2 + rank)[None, :] == slots[:, None])
    take = jnp.sum(jnp.where(sent, local_slot[None, :], 0), axis=1)
    rows = jnp.arange(incoming, dtype=jnp.int32)
    placed = (target == self_index)[None, :] & (arrival[None, :] == rows[:, None])
    put = jnp.sum(jnp.where(placed, (source * 2 + rank + 1)[None, :], 0), axis=1) - 1
    here = jnp.arange(branches_here, dtype=jnp.int32)
    leaving = jnp.sum((local_slot[None, :] == here[:, None]).astype(jnp.int32), axis=1)
    stay = (leaving == 0).astype(jnp.int32)
    return take, put, stay


def on_device(queries, prompt_cache, tails, fresh, residual, out_proj, lengths, prompt_of, moves):
    groups = lax.axis_size("dp")
    self_index = lax.axis_index("dp")
    branches_here = queries.shape[0]
    take, put, stay = routing(moves, self_index, branches_here, groups, groups - 1)

    def across(values):
        return jnp.broadcast_to(values[:, None], (branches_here, HEAD))

    rows, arrived_rows, arrived_tails, home = block(
        take,
        stay,
        lengths,
        jnp.transpose(queries, (1, 0, 2)),
        jnp.transpose(residual, (1, 0, 2)),
        fresh,
        across(lengths),
        across(prompt_of - self_index * prompt_cache.shape[0]),
        tails,
        prompt_cache,
        out_proj,
    )
    mixed, tails_out = place(
        put,
        across(stay),
        rows,
        arrived_rows.reshape((groups * 2,) + arrived_rows.shape[2:]),
        home,
        arrived_tails.reshape((groups * 2,) + arrived_tails.shape[2:]),
    )
    return (jnp.transpose(mixed, (1, 0, 2)), tails_out)


def solution(mesh):
    in_specs = (
        P("dp", None, "tensor"),
        P("dp", None, None, "tensor"),
        P("dp", None, None, "tensor"),
        P("dp", None, None, "tensor"),
        P("dp", None, "tensor"),
        P("tensor", None),
        P("dp"),
        P("dp"),
        P(),
    )
    out_specs = (P("dp", None, "tensor"), P("dp", None, None, "tensor"))
    return jax.shard_map(
        on_device, mesh=mesh, in_specs=in_specs, out_specs=out_specs, check_vma=False
    )
```

time: 185 us -> 79.4 us (0.43)
  Pallas kernels: 0 us -> 68.2 us
  matrix products: 61.9 us -> 0 us
  waiting for transfers between devices: 61.2 us -> 0 us
  starting transfers between devices: 24.5 us -> 0 us
  between operations: 14.4 us -> 0.68 us
  other arithmetic: 15.9 us -> 2.32 us
    pallas_call x0 -> x2, Pallas kernels: none -> 68.2 us  [the longest x1 64.7 us: block(): pl.pallas_call(body, out_shape=[jax.ShapeDtypeStruct(queries.shape, kind)...]
    dot_general x18 -> x0, matrix products: 61.9 us -> none  [the longest x2 22.8 us: attend(): jnp.einsum('bnkgd,tkd->bnkgt', grouped, keys_here, preferred_element_type...]
    all_to_all x3 -> x0, waiting for transfers between devices: 61.2 us -> none  [the longest x1 48.7 us: on_device(): lax.all_to_all(route_rows(pack_matrix, tails_written), 'dp', split_axis=0...]
    all_to_all x3 -> x0, starting transfers between devices: 24.2 us -> none  [the longest x1 11.3 us: on_device(): lax.all_to_all(route_rows(pack_matrix, heads_out), 'dp', split_axis=0, co...]
    reduce_sum x5 -> x4, other arithmetic: 11 us -> 0.82 us  [the longest x1 0.45 us: routing(): arrival = jnp.sum(same_target.astype(jnp.int32), axis=1)]
    unnamed x21 -> x12, local copies, waits for them, and re-layouts: 2.44 us -> 6.97 us
    concatenate x1 -> x0, other arithmetic: 2.36 us -> none  [on_device(): jnp.concatenate([keep_rows(staying, tails_written), route_rows(place_matr...]
    reshape x8 -> x0, local copies, waits for them, and re-layouts: 2.02 us -> none  [the longest x6 1.88 us: route_rows(): return moved.reshape((matrix.shape[0],) + rows.shape[1:])]
  transfers between devices with their start and end apart: 4 -> 0, of which waited for: 3 -> 0; matrix products, arithmetic and copies ran while one was open for 9% -> 0% of each run, Pallas kernels for 0% -> 0%
where the time goes in v1:
time: 79.4 us; the launch traced here: 79 us
  Pallas kernels  68.2 us (86%)
  local copies, waits for them, and re-layouts  7.85 us (10%)
  other arithmetic  2.32 us (3%)
    pallas_call x1, Pallas kernels, block(): pl.pallas_call(body, out_shape=[jax.ShapeDtypeStruct(queries.shape, kind)...  64.7 us
    unnamed x12, local copies, waits for them, and re-layouts  6.97 us
    pallas_call x1, Pallas kernels, place(): pl.pallas_call(place_kernel, out_shape=[jax.ShapeDtypeStruct((new_count,...  3.54 us

profile of v1, /device:TPU:16, one launch (start us, length us, event | category | flops | bytes accessed | tf_op | source)
XLA Modules:
  0.0 79.0 jit_solution(5543578377551564062)
XLA Ops:
  0.6 0.7 broadcast_subtract_fusion
  1.3 0.8 %slice_subtract_fusion = (s32[496,1]{0,1:T(1,128)S(1)}, s32[496,1]{0,1:T(1,128)S(1)}, s32[496,1]{0,1:T(1,128)S(1)}) fusion(s32[496,3]{0,1:T(4,128)} %param.17, s32[]{:T(128)S(6)} %mul.21), kind=kLoop, calls=%fused_computation.13 | loop fusion | flops 496 | bytes 11908 | tf_op jit(solution)/shard_map/sub | solution.py:525
  2.1 0.1 convert_reduce_fusion.2
  2.2 0.4 convert_reduce_fusion.1
  2.7 0.1 select_reduce_fusion.1
  2.8 0.1 select_reduce_fusion.refs_0_
  3.0 0.1 broadcast_in_dim.36.refs_7_
  3.0 0.1 broadcast_in_dim.32.keep_ref
  3.1 0.7 broadcast_in_dim.35.refs_6_
  3.9 0.0 copy-start.2
  3.9 0.7 copy-done.2
  4.5 0.0 copy-start.3
  4.5 1.0 %copy-done.3 = bf16[96,3,512]{2,0,1:T(8,128)(2,1)S(1)} copy-done((bf16[96,3,512]{2,0,1:T(8,128)(2,1)S(1)}, bf16[96,3,512]{2,0,1:T(8,128)(2,1)}, u32[]{:S(2)}) %copy-start.3) | copy-done | bytes 294936
  5.5 0.0 copy-start.4
  5.5 1.0 %copy-done.4 = bf16[96,3,512]{2,0,1:T(8,128)(2,1)S(1)} copy-done((bf16[96,3,512]{2,0,1:T(8,128)(2,1)S(1)}, bf16[96,3,512]{2,0,1:T(8,128)(2,1)}, u32[]{:S(2)}) %copy-start.4) | copy-done | bytes 294936
  6.4 0.0 copy-start.5
  6.5 0.9 %copy-done.5 = bf16[96,3,2,128]{3,2,1,0:T(2,128)(2,1)S(1)} copy-done((bf16[96,3,2,128]{3,2,1,0:T(2,128)(2,1)S(1)}, bf16[96,3,2,128]{3,2,1,0:T(2,128)(2,1)}, u32[]{:S(2)}) %copy-start.5) | copy-done | bytes 147480
  7.4 64.7 %shard_map.104 = (bf16[3,96,512]{2,1,0:T(8,128)(2,1)S(1)}, bf16[32,2,16,128]{3,2,1,0:T(8,128)(2,1)S(1)}, bf16[32,2,2,64,128]{4,3,2,1,0:T(8,128)(2,1)}, bf16[96,2,64,128]{3,2,1,0:T(8,128)(2,1)}) custom-call(s32[64]{0:T(128)S(1)} %select_reduce_fusion.refs_0_, s32[96]{0:T(128)S(1)} %copy-done.2, s32[96]{0:T(128)S(1)} %compare_convert_fusion.refs_2_, ...), custom_call_target="tpu_custom_call" | custom-call | flops 4831838208 | bytes 20971520 | tf_op jit(solution)/shard_map/pallas_call | solution.py:388
  72.0 0.0 copy-start
  72.0 1.9 %copy-done = bf16[96,2,64,128]{3,2,1,0:T(8,128)(2,1)S(1)} copy-done((bf16[96,2,64,128]{3,2,1,0:T(8,128)(2,1)S(1)}, bf16[96,2,64,128]{3,2,1,0:T(8,128)(2,1)}, u32[]{:S(2)}) %copy-start) | copy-done | bytes 3145752
  73.9 0.0 copy-start.1
  73.9 1.6 %copy-done.1 = bf16[32,2,2,64,128]{4,3,2,1,0:T(8,128)(2,1)S(1)} copy-done((bf16[32,2,2,64,128]{4,3,2,1,0:T(8,128)(2,1)S(1)}, bf16[32,2,2,64,128]{4,3,2,1,0:T(8,128)(2,1)}, u32[]{:S(2)}) %copy-start.1) | copy-done | bytes 2097176
  75.5 3.5 %shard_map.105 = (bf16[3,127,512]{2,1,0:T(8,128)(2,1)}, bf16[127,2,64,128]{3,2,1,0:T(8,128)(2,1)}) custom-call(s32[31]{0:T(128)S(1)} %broadcast_add_fusion.take_ref, s32[96,128]{1,0:T(8,128)S(1)} %broadcast_in_dim.32.keep_ref, bf16[3,96,512]{2,1,0:T(8,128)(2,1)S(1)} %get-tuple-element.8.rows_ref, bf16[64,16,128]{2,1,0:T(8,128)(2,1)S(1)} %bitcast.9, ...), custom_call_target="tpu_custom_call" | custom-call | tf_op jit(solution)/shard_map/pallas_call | solution.py:500
  (4 shorter events, 0.0 us)
Async XLA Ops:
  3.9 0.7 copy-start.2
  4.5 1.0 %copy-start.3 = (bf16[96,3,512]{2,0,1:T(8,128)(2,1)S(1)}, bf16[96,3,512]{2,0,1:T(8,128)(2,1)}, u32[]{:S(2)}) copy-start(bf16[96,3,512]{2,0,1:T(8,128)(2,1)} %param.9) | copy-start | bytes 884740
  5.5 1.0 %copy-start.4 = (bf16[96,3,512]{2,0,1:T(8,128)(2,1)S(1)}, bf16[96,3,512]{2,0,1:T(8,128)(2,1)}, u32[]{:S(2)}) copy-start(bf16[96,3,512]{2,0,1:T(8,128)(2,1)} %param.13) | copy-start | bytes 884740
  6.4 0.9 %copy-start.5 = (bf16[96,3,2,128]{3,2,1,0:T(2,128)(2,1)S(1)}, bf16[96,3,2,128]{3,2,1,0:T(2,128)(2,1)}, u32[]{:S(2)}) copy-start(bf16[96,3,2,128]{3,2,1,0:T(2,128)(2,1)} %refs_5_.1) | copy-start | bytes 442372
  72.0 1.9 %copy-start = (bf16[96,2,64,128]{3,2,1,0:T(8,128)(2,1)S(1)}, bf16[96,2,64,128]{3,2,1,0:T(8,128)(2,1)}, u32[]{:S(2)}) copy-start(bf16[96,2,64,128]{3,2,1,0:T(8,128)(2,1)} %get-tuple-element.10.home_ref) | copy-start | bytes 9437188
  73.9 1.6 %copy-start.1 = (bf16[32,2,2,64,128]{4,3,2,1,0:T(8,128)(2,1)S(1)}, bf16[32,2,2,64,128]{4,3,2,1,0:T(8,128)(2,1)}, u32[]{:S(2)}) copy-start(bf16[32,2,2,64,128]{4,3,2,1,0:T(8,128)(2,1)} %get-tuple-element.11) | copy-start | bytes 6291460

commit v2 on v1

--- a/solution.py
+++ b/solution.py
@@ -14,6 +14,7 @@
 CORES = 2
 ROW = 16
 MIB = 1 << 20
+HOME_PARTS = 6
 MESH = pl.DeviceIdType.MESH
 
 
@@ -122,17 +123,57 @@
             heads[i, pl.ds(first, GROUP), h * HEAD : (h + 1) * HEAD] = result[at : at + GROUP]
 
 
+def find_slots(me, groups, branches_here, moves, slot_table, keep_rows):
+    branch, source, target = (moves[at : at + 1] for at in range(3))
+    entries = moves.shape[1]
+    group = lax.broadcasted_iota(jnp.int32, (groups, entries), 0)
+    entry = lax.broadcasted_iota(jnp.int32, (groups, entries), 1)
+    local = branch - me * branches_here
+    far = entries * HEAD
+    code = jnp.where((source == me) & (target == group), entry * HEAD + local, -1)
+    last = jnp.max(code, axis=1, keepdims=True)
+    first = jnp.min(jnp.where(code >= 0, code, far), axis=1, keepdims=True)
+    sent = [jnp.where(first < far, first % HEAD, 0), jnp.where(last >= 0, last % HEAD, 0)]
+    here = target == me
+    code = jnp.where(here & (source == group), entry, -1)
+    last = jnp.max(code, axis=1, keepdims=True)
+    first = jnp.min(jnp.where(code >= 0, code, entries), axis=1, keepdims=True)
+
+    def arrival(at):
+        return jnp.sum(jnp.where(here & (entry < at), 1, 0), axis=1, keepdims=True)
+
+    arrive = [
+        jnp.where(last >= 0, arrival(first), -1),
+        jnp.where(last > first, arrival(last), -1),
+    ]
+    column = lax.broadcasted_iota(jnp.int32, slot_table.shape, 1)
+    table = jnp.broadcast_to(arrival(entries), slot_table.shape)
+    for at, value in enumerate(sent + arrive):
+        table = jnp.where(column == at, value, table)
+    slot_table[...] = table
+    row = lax.broadcasted_iota(jnp.int32, (branches_here, entries), 0)
+    gone = jnp.where((source == me) & (local == row), 1, 0)
+    gone = jnp.max(gone, axis=1, keepdims=True)
+    keep_rows[...] = jnp.broadcast_to(1 - gone, keep_rows.shape)
+
+
+def spread(scalars, rows, base=0):
+    def step(at, carry):
+        rows[pl.ds(at, 1)] = jnp.full((1, rows.shape[1]), scalars[at] - base, jnp.int32)
+        return carry
+
+    lax.fori_loop(0, rows.shape[0], step, 0)
+
+
 def block_kernel(
     groups,
     chips,
-    take_ref,
-    branch_length_ref,
-    stay_ref,
-    query_ref,
-    residual_ref,
-    fresh_ref,
-    length_ref,
-    second_ref,
+    lengths_in,
+    prompt_of_in,
+    moves_in,
+    query_in,
+    residual_in,
+    fresh_in,
     tails_in,
     cache_in,
     proj_in,
@@ -140,6 +181,18 @@
     arrived_rows,
     arrived_tails,
     home_out,
+    slots_out,
+    branch_length_ref,
+    branch_prompt_ref,
+    moves,
+    slot_table,
+    slot_scalars,
+    keep_rows,
+    length_ref,
+    second_ref,
+    query_ref,
+    residual_ref,
+    fresh_ref,
     tails,
     cache,
     proj,
@@ -186,12 +239,20 @@
         )
         return carry
 
-    load_tails = pltpu.make_async_copy(tails_in, tails, load_sems.at[0])
-    load_cache = pltpu.make_async_copy(cache_in, cache, load_sems.at[1])
-    load_proj = pltpu.make_async_copy(proj_in, proj, load_sems.at[2])
+    load_lengths = pltpu.make_async_copy(lengths_in, branch_length_ref, load_sems.at[8])
+    load_prompts = pltpu.make_async_copy(prompt_of_in, branch_prompt_ref, load_sems.at[9])
+    load_moves = pltpu.make_async_copy(moves_in, moves, load_sems.at[0])
+    load_tails = pltpu.make_async_copy(tails_in, tails, load_sems.at[1])
+    load_fresh = pltpu.make_async_copy(fresh_in, fresh_ref, load_sems.at[2])
+    load_query = pltpu.make_async_copy(query_in, query_ref, load_sems.at[3])
+    load_residual = pltpu.make_async_copy(residual_in, residual_ref, load_sems.at[4])
+    load_cache = pltpu.make_async_copy(cache_in, cache, load_sems.at[5])
+    load_proj = pltpu.make_async_copy(proj_in, proj, load_sems.at[6])
+    load_moves.start()
     load_tails.start()
-    load_cache.start()
-    load_proj.start()
+    load_fresh.start()
+    load_lengths.start()
+    load_prompts.start()
     lax.fori_loop(1, groups, greet, 0)
     pl.semaphore_signal(barrier, inc=1, device_id=(me, other), device_id_type=MESH)
     for step in range(1, chips):
@@ -202,10 +263,22 @@
             device_id_type=MESH,
         )
 
+    load_query.start()
+    load_residual.start()
+    load_cache.start()
+    load_proj.start()
+    load_moves.wait()
+    find_slots(me, groups, branches_here, moves, slot_table, keep_rows)
+    load_slots = pltpu.make_async_copy(slot_table, slot_scalars, load_sems.at[7])
+    load_slots.start()
+    load_slots.wait()
     load_tails.wait()
+    load_fresh.wait()
+    load_lengths.wait()
+    load_prompts.wait()
 
     def pack(slot, carry):
-        branch = take_ref[slot]
+        branch = slot_scalars[slot // 2, slot % 2]
         length = branch_length_ref[branch]
         for kind in range(2):
             staged[slot // 2, slot % 2, kind] = written_rows(
@@ -270,6 +343,13 @@
         return carry
 
     lax.fori_loop(0, branches_here, widen, 0)
+    spread(branch_length_ref, length_ref)
+    spread(branch_prompt_ref, second_ref, me * cache.shape[0])
+    store_slots = pltpu.make_async_copy(slot_table, slots_out, load_sems.at[0])
+    store_slots.start()
+    store_slots.wait()
+    load_query.wait()
+    load_residual.wait()
     load_cache.wait()
     load_proj.wait()
 
@@ -304,7 +384,8 @@
         for i in range(new_count):
             rows = summed[i * spans : (i + 1) * spans]
             rows += residual_ref[i, pl.ds(first, spans)].astype(jnp.float32)
-            rows_out[i, pl.ds(first, spans)] = rows.astype(rows_out.dtype)
+            keep = jnp.concatenate([keep_rows[pl.ds(first, spans)]] * (width // HEAD), axis=1) > 0
+            rows_out[i, pl.ds(first, spans)] = jnp.where(keep, rows, 0.0).astype(rows_out.dtype)
             for at in range(0, width, HEAD):
                 wide_rows[pl.ds(first, spans), i * (width // HEAD) + at // HEAD] = rows[
                     :, at : at + HEAD
@@ -331,11 +412,12 @@
     exchange(chunks - 1)
 
     def settle(branch, carry):
-        keep = stay_ref[branch] > 0
+        keep = jnp.broadcast_to(keep_rows[pl.ds(branch, 1)], tails.shape[2:]) > 0
         length = branch_length_ref[branch]
         for kind in range(2):
             rows = written_rows(tails[branch, kind], fresh_of(fresh_ref, branch, kind), length)
-            tails[branch, kind] = jnp.where(keep, rows, jnp.zeros_like(rows))
+            rows = jnp.where(keep, rows.astype(jnp.float32), 0.0)
+            tails[branch, kind] = rows.astype(tails.dtype)
         return carry
 
     def finish_chunk(chunk, carry):
@@ -346,7 +428,9 @@
     lax.fori_loop(0, chunks, finish_chunk, 0)
 
     def pack_rows(slot, carry):
-        staged_rows[slot // 2, slot % 2] = wide_rows[take_ref[slot]].astype(staged_rows.dtype)
+        staged_rows[slot // 2, slot % 2] = wide_rows[
+            slot_scalars[slot // 2, slot % 2]
+        ].astype(staged_rows.dtype)
         return carry
 
     lax.fori_loop(0, groups * 2, pack_rows, 0)
@@ -357,7 +441,7 @@
 
     lax.fori_loop(1, groups, send_rows, 0)
     lax.fori_loop(0, branches_here, settle, 0)
-    store_home = pltpu.make_async_copy(tails, home_out, load_sems.at[3])
+    store_home = pltpu.make_async_copy(tails, home_out, load_sems.at[1])
     store_home.start()
     store_home.wait()
 
@@ -369,14 +453,14 @@
     lax.fori_loop(1, groups, drain, 0)
 
 
-def block(take, stay, lengths, queries, residual, fresh, length_rows, second, tails, cache, proj):
+def block(*arrays):
+    lengths, prompt_of, moves, queries, residual, fresh, tails, cache, proj = arrays
     groups, chips = lax.axis_size("dp"), lax.axis_size("tensor") // CORES
     new_count, branches_here, width = queries.shape
     spans = GROUP * TILES
     chunks = branches_here // spans
     rows = new_count * (width // HEAD) * GROUP
     kind = queries.dtype
-    smem = pl.BlockSpec(memory_space=pltpu.SMEM)
     vmem = pl.BlockSpec(memory_space=pltpu.VMEM)
     hbm = pl.BlockSpec(memory_space=pl.ANY)
     flops = 8 * new_count * branches_here * (width // HEAD) * cache.shape[2] * HEAD
@@ -388,14 +472,26 @@
     return pl.pallas_call(
         body,
         out_shape=[
-            jax.ShapeDtypeStruct(queries.shape, kind),
-            jax.ShapeDtypeStruct((groups, 2, ROW, HEAD), kind),
-            jax.ShapeDtypeStruct((groups, 2) + tails.shape[1:], kind),
-            jax.ShapeDtypeStruct(tails.shape, kind),
+            pltpu.VMEM(queries.shape, kind),
+            pltpu.VMEM((groups, 2, ROW, HEAD), kind),
+            pltpu.VMEM((groups, 2) + tails.shape[1:], kind),
+            pltpu.VMEM(tails.shape, kind),
+            pltpu.VMEM((groups, HEAD), jnp.int32),
         ],
-        in_specs=[smem] * 3 + [vmem] * 5 + [hbm] * 3,
-        out_specs=[vmem, hbm, hbm, hbm],
+        in_specs=[pl.BlockSpec(memory_space=pltpu.HBM)] * 9,
+        out_specs=[vmem, hbm, hbm, hbm, hbm],
         scratch_shapes=[
+            pltpu.SMEM(lengths.shape, jnp.int32),
+            pltpu.SMEM(prompt_of.shape, jnp.int32),
+            pltpu.VMEM(moves.shape, jnp.int32),
+            pltpu.VMEM((groups, HEAD), jnp.int32),
+            pltpu.SMEM((groups, HEAD), jnp.int32),
+            pltpu.VMEM((branches_here, HEAD), jnp.int32),
+            pltpu.VMEM((branches_here, HEAD), jnp.int32),
+            pltpu.VMEM((branches_here, HEAD), jnp.int32),
+            pltpu.VMEM(queries.shape, kind),
+            pltpu.VMEM(residual.shape, kind),
+            pltpu.VMEM(fresh.shape, kind),
             pltpu.VMEM(tails.shape, kind),
             pltpu.VMEM(cache.shape, kind),
             pltpu.VMEM(proj.shape, kind),
@@ -410,7 +506,7 @@
             pltpu.VMEM((chunks, chips - 1, new_count * spans, width), kind),
             pltpu.VMEM((chunks, chips - 1, new_count * spans, width), kind),
             pltpu.VMEM((branches_here, ROW, HEAD), jnp.float32),
-            dma((4,)),
+            dma((10,)),
             dma((groups,)),
             dma((groups,)),
             dma((groups,)),
@@ -424,74 +520,93 @@
             flops=flops, bytes_accessed=20 * MIB, transcendentals=flops // 1024
         ),
         compiler_params=pltpu.CompilerParams(
-            collective_id=0, has_side_effects=True, vmem_limit_bytes=52 * MIB
+            collective_id=0, has_side_effects=True, vmem_limit_bytes=46 * MIB
         ),
-    )(take, lengths, stay, queries, residual, fresh, length_rows, second, tails, cache, proj)
+    )(*(pltpu.with_memory_space_constraint(array, pltpu.HBM) for array in arrays))
 
 
 def place_kernel(
-    take_ref,
-    keep_ref,
-    rows_ref,
-    arrived_rows_ref,
-    home_ref,
-    arrived_ref,
+    slots_ref,
+    rows_in,
+    arrived_rows_in,
+    home_in,
+    arrived_in,
     mixed_ref,
     out_ref,
+    rows,
+    arrived_rows,
     blank,
     stage,
     sems,
-    home_sem,
+    load_sems,
 ):
-    incoming = take_ref.shape[0]
-    new_count, first, width = rows_ref.shape
+    incoming = sems.shape[0]
+    new_count, first, width = rows.shape
     lines = new_count * (width // HEAD)
-    copy_home = pltpu.make_async_copy(home_ref, out_ref.at[pl.ds(0, first)], home_sem)
-    copy_home.start()
+    parts = load_sems.shape[0] - 2
+    share = first // parts
+    load_rows = pltpu.make_async_copy(rows_in, rows, load_sems.at[0])
+    load_arrived = pltpu.make_async_copy(arrived_rows_in, arrived_rows, load_sems.at[1])
+
+    def home_copy(part):
+        at = pl.ds(part * share, share)
+        return pltpu.make_async_copy(home_in.at[at], out_ref.at[at], load_sems.at[2 + part])
+
+    def row_copy(source, row):
+        return pltpu.make_async_copy(source, out_ref.at[first + row], sems.at[row])
+
+    load_arrived.start()
+    load_rows.start()
+    for part in range(parts):
+        home_copy(part).start()
     blank[...] = jnp.zeros_like(blank)
-
-    def start(row, carry):
-        source = take_ref[row]
-
-        @pl.when(source >= 0)
+    stage[...] = jnp.zeros_like(stage)
+    count = slots_ref[0, 4]
+
+    def start(slot, carry):
+        row = slots_ref[slot // 2, 2 + slot % 2]
+
+        @pl.when(row >= 0)
         def _():
-            pltpu.make_async_copy(
-                arrived_ref.at[source], out_ref.at[first + row], sems.at[row]
-            ).start()
-
-        @pl.when(source < 0)
+            row_copy(arrived_in.at[slot], row).start()
+
+        return carry
+
+    def clear(row, carry):
+        row_copy(blank, row).start()
+        return carry
+
+    def stage_row(slot, carry):
+        row = slots_ref[slot // 2, 2 + slot % 2]
+
+        @pl.when(row >= 0)
         def _():
-            pltpu.make_async_copy(blank, out_ref.at[first + row], sems.at[row]).start()
-
-        return carry
-
-    def stage_row(row, carry):
-        source = take_ref[row]
-        value = arrived_rows_ref[jnp.maximum(source, 0)].astype(jnp.float32)
-        value = jnp.where(source >= 0, value, 0.0)
-        for line in range(lines):
-            stage[line, pl.ds(row, 1)] = value[line : line + 1]
+            value = arrived_rows[slot].astype(jnp.float32)
+            for line in range(lines):
+                stage[line, pl.ds(row, 1)] = value[line : line + 1]
+
         return carry
 
     def done(row, carry):
-        pltpu.make_async_copy(blank, out_ref.at[first + row], sems.at[row]).wait()
-        return carry
-
-    lax.fori_loop(0, incoming, start, 0)
-    lax.fori_loop(0, incoming, stage_row, 0)
-    keep = jnp.concatenate([keep_ref[...]] * (width // HEAD), axis=1) > 0
+        row_copy(blank, row).wait()
+        return carry
+
+    lax.fori_loop(0, arrived_in.shape[0], start, 0)
+    lax.fori_loop(count, incoming, clear, 0)
+    load_arrived.wait()
+    lax.fori_loop(0, arrived_in.shape[0], stage_row, 0)
+    load_rows.wait()
     for i in range(new_count):
-        rows = rows_ref[i]
-        mixed_ref[i, :first] = jnp.where(keep, rows, jnp.zeros_like(rows))
+        mixed_ref[i, :first] = rows[i]
         for at in range(0, width, HEAD):
             line = i * (width // HEAD) + at // HEAD
             mixed_ref[i, first:, at : at + HEAD] = stage[line, :incoming].astype(mixed_ref.dtype)
     lax.fori_loop(0, incoming, done, 0)
-    copy_home.wait()
-
-
-def place(take, keep, rows, arrived_rows, home, arrived):
-    incoming = take.shape[0]
+    for part in range(parts):
+        home_copy(part).wait()
+
+
+def place(slot_table, rows, arrived_rows, home, arrived, incoming):
     new_count, branches_here, width = rows.shape
     slots = branches_here + incoming
     smem = pl.BlockSpec(memory_space=pltpu.SMEM)
@@ -503,67 +618,40 @@
             jax.ShapeDtypeStruct((new_count, slots, width), rows.dtype),
             jax.ShapeDtypeStruct((slots,) + home.shape[1:], home.dtype),
         ],
-        in_specs=[smem, vmem, vmem, vmem, hbm, hbm],
+        in_specs=[smem] + [hbm] * 4,
         out_specs=[vmem, hbm],
         scratch_shapes=[
+            pltpu.VMEM(rows.shape, rows.dtype),
+            pltpu.VMEM(arrived_rows.shape, rows.dtype),
             pltpu.VMEM(home.shape[1:], home.dtype),
             pltpu.VMEM((new_count * (width // HEAD), incoming + 1, HEAD), jnp.float32),
             pltpu.SemaphoreType.DMA((incoming,)),
-            pltpu.SemaphoreType.DMA(()),
+            pltpu.SemaphoreType.DMA((2 + HOME_PARTS,)),
         ],
         compiler_params=pltpu.CompilerParams(vmem_limit_bytes=8 * MIB),
-    )(take, keep, rows, arrived_rows, home, arrived)
-
-
-def routing(moves, self_index, branches_here, groups, incoming):
-    branch_ids, source, target = moves[:, 0], moves[:, 1], moves[:, 2]
-    entries = jnp.arange(moves.shape[0], dtype=jnp.int32)
-    earlier = entries[None, :] < entries[:, None]
-    same_target = earlier & (target[None, :] == target[:, None])
-    arrival = jnp.sum(same_target.astype(jnp.int32), axis=1)
-    rank = jnp.sum((same_target & (source[None, :] == source[:, None])).astype(jnp.int32), axis=1)
-    local_slot = branch_ids - self_index * branches_here
-    slots = jnp.arange(groups * 2, dtype=jnp.int32)
-    sent = (source == self_index)[None, :] & ((target * 2 + rank)[None, :] == slots[:, None])
-    take = jnp.sum(jnp.where(sent, local_slot[None, :], 0), axis=1)
-    rows = jnp.arange(incoming, dtype=jnp.int32)
-    placed = (target == self_index)[None, :] & (arrival[None, :] == rows[:, None])
-    put = jnp.sum(jnp.where(placed, (source * 2 + rank + 1)[None, :], 0), axis=1) - 1
-    here = jnp.arange(branches_here, dtype=jnp.int32)
-    leaving = jnp.sum((local_slot[None, :] == here[:, None]).astype(jnp.int32), axis=1)
-    stay = (leaving == 0).astype(jnp.int32)
-    return take, put, stay
+    )(slot_table, rows, arrived_rows, home, arrived)
 
 
 def on_device(queries, prompt_cache, tails, fresh, residual, out_proj, lengths, prompt_of, moves):
     groups = lax.axis_size("dp")
-    self_index = lax.axis_index("dp")
-    branches_here = queries.shape[0]
-    take, put, stay = routing(moves, self_index, branches_here, groups, groups - 1)
-
-    def across(values):
-        return jnp.broadcast_to(values[:, None], (branches_here, HEAD))
-
-    rows, arrived_rows, arrived_tails, home = block(
-        take,
-        stay,
+    rows, arrived_rows, arrived_tails, home, slot_table = block(
         lengths,
+        prompt_of,
+        jnp.transpose(moves),
         jnp.transpose(queries, (1, 0, 2)),
         jnp.transpose(residual, (1, 0, 2)),
         fresh,
-        across(lengths),
-        across(prompt_of - self_index * prompt_cache.shape[0]),
         tails,
         prompt_cache,
         out_proj,
     )
     mixed, tails_out = place(
-        put,
-        across(stay),
+        slot_table,
         rows,
         arrived_rows.reshape((groups * 2,) + arrived_rows.shape[2:]),
         home,
         arrived_tails.reshape((groups * 2,) + arrived_tails.shape[2:]),
+        groups - 1,
     )
     return (jnp.transpose(mixed, (1, 0, 2)), tails_out)
 

time: 79.4 us -> 70 us (0.88)
  local copies, waits for them, and re-layouts: 7.85 us -> 0 us
  other arithmetic: 2.32 us -> 0 us
  Pallas kernels: 68.2 us -> 69.2 us
    unnamed x12 -> x0, local copies, waits for them, and re-layouts: 6.97 us -> none
    sub x3 -> x0, other arithmetic: 1.48 us -> none  [the longest x1 0.81 us: routing(): local_slot = branch_ids - self_index * branches_here]
    pallas_call x1, Pallas kernels: 3.54 us -> 4.54 us  [place(): pl.pallas_call(place_kernel, out_shape=[jax.ShapeDtypeStruct((new_count,...]
    broadcast_in_dim x3 -> x0, local copies, waits for them, and re-layouts: 0.89 us -> none  [across(): return jnp.broadcast_to(values[:, None], (branches_here, HEAD))]
    reduce_sum x4 -> x0, other arithmetic: 0.82 us -> none  [the longest x1 0.45 us: routing(): arrival = jnp.sum(same_target.astype(jnp.int32), axis=1)]
where the time goes in v2:
time: 70 us; the launch traced here: 69.8 us
  Pallas kernels  69.2 us (99%)
    pallas_call x1, Pallas kernels, block(): pl.pallas_call(body, out_shape=[pltpu.VMEM(queries.shape, kind), pltpu.VM...  64.7 us
    pallas_call x1, Pallas kernels, place(): pl.pallas_call(place_kernel, out_shape=[jax.ShapeDtypeStruct((new_count,...  4.54 us

profile of v2, /device:TPU:16, one launch (start us, length us, event | category | flops | bytes accessed | tf_op | source)
XLA Modules:
  0.0 69.8 jit_solution(4955969336727694597)
XLA Ops:
  0.6 64.7 %shard_map.104 = (bf16[3,96,512]{2,1,0:T(8,128)(2,1)S(1)}, bf16[32,2,16,128]{3,2,1,0:T(8,128)(2,1)S(1)}, bf16[32,2,2,64,128]{4,3,2,1,0:T(8,128)(2,1)S(1)}, bf16[...) custom-call(s32[96]{0:T(128)} %refs_0_.1, s32[96]{0:T(128)} %refs_1_.1, s32[3,496]{1,0:T(4,128)} %bitcast.11, ...), custom_call_target="tpu_custom_call" | custom-call | flops 4831838208 | bytes 20971520 | tf_op jit(solution)/shard_map/pallas_call | solution.py:472
  65.3 4.5 %shard_map.105 = (bf16[3,127,512]{2,1,0:T(8,128)(2,1)}, bf16[127,2,64,128]{3,2,1,0:T(8,128)(2,1)}) custom-call(s32[32,128]{1,0:T(8,128)S(1)} %get-tuple-element.9.slots_ref, bf16[3,96,512]{2,1,0:T(8,128)(2,1)S(1)} %get-tuple-element.10.rows_in, bf16[64,16,128]{2,1,0:T(8,128)(2,1)S(1)} %bitcast.7, bf16[96,2,64,128]{3,2,1,0:T(8,128)(2,1)S(1)} %get-tuple-element.12.home_in, ...), custom_call_target="tpu_custom_call" | custom-call | tf_op jit(solution)/shard_map/pallas_call | solution.py:615

commit v3 on v2

--- a/solution.py
+++ b/solution.py
@@ -14,8 +14,12 @@
 CORES = 2
 ROW = 16
 MIB = 1 << 20
-HOME_PARTS = 6
+PARTS = 4
 MESH = pl.DeviceIdType.MESH
+
+
+def wrapped(index, size):
+    return jnp.where(index >= size, index - size, index)
 
 
 def written_rows(rows, fresh, length):
@@ -142,13 +146,20 @@
     def arrival(at):
         return jnp.sum(jnp.where(here & (entry < at), 1, 0), axis=1, keepdims=True)
 
-    arrive = [
-        jnp.where(last >= 0, arrival(first), -1),
-        jnp.where(last > first, arrival(last), -1),
-    ]
+    square = (groups, groups)
+    row = lax.broadcasted_iota(jnp.int32, square, 0)
+    column = lax.broadcasted_iota(jnp.int32, square, 1)
+
+    def flat(value):
+        return jnp.sum(jnp.where(row == column, value, 0), axis=0, keepdims=True)
+
+    once = flat(jnp.where(last >= 0, arrival(first), -1))
+    twice = flat(jnp.where(last > first, arrival(last), -1))
+    slot = jnp.where(once == row, column * 2, jnp.where(twice == row, column * 2 + 1, -1))
+    sent.append(jnp.max(slot, axis=1, keepdims=True))
     column = lax.broadcasted_iota(jnp.int32, slot_table.shape, 1)
-    table = jnp.broadcast_to(arrival(entries), slot_table.shape)
-    for at, value in enumerate(sent + arrive):
+    table = jnp.zeros(slot_table.shape, jnp.int32)
+    for at, value in enumerate(sent):
         table = jnp.where(column == at, value, table)
     slot_table[...] = table
     row = lax.broadcasted_iota(jnp.int32, (branches_here, entries), 0)
@@ -177,11 +188,11 @@
     tails_in,
     cache_in,
     proj_in,
-    rows_out,
+    mixed_out,
+    tails_out,
     arrived_rows,
     arrived_tails,
-    home_out,
-    slots_out,
+    stage,
     branch_length_ref,
     branch_prompt_ref,
     moves,
@@ -226,10 +237,10 @@
     chunks = branches_here // spans
 
     def peer_of(step):
-        return lax.rem(me + step, groups)
+        return wrapped(me + step, groups)
 
     def chip_of(step):
-        return lax.rem(chip + step, chips)
+        return wrapped(chip + step, chips)
 
     barrier = pltpu.get_barrier_semaphore()
 
@@ -277,22 +288,23 @@
     load_lengths.wait()
     load_prompts.wait()
 
-    def pack(slot, carry):
-        branch = slot_scalars[slot // 2, slot % 2]
-        length = branch_length_ref[branch]
-        for kind in range(2):
-            staged[slot // 2, slot % 2, kind] = written_rows(
-                tails[branch, kind], fresh_of(fresh_ref, branch, kind), length
-            )
-        return carry
-
-    lax.fori_loop(0, groups * 2, pack, 0)
+    def pack(group, carry):
+        for pick in range(2):
+            branch = slot_scalars[group, pick]
+            length = branch_length_ref[branch]
+            for kind in range(2):
+                staged[group * 2 + pick, kind] = written_rows(
+                    tails[branch, kind], fresh_of(fresh_ref, branch, kind), length
+                )
+        return carry
+
+    lax.fori_loop(0, groups, pack, 0)
     pl.semaphore_wait(barrier, groups - 1 + 1 + chips - 1)
 
     def tail_copy(step):
         return pltpu.make_async_remote_copy(
-            src_ref=staged.at[peer_of(step)],
-            dst_ref=arrived_tails.at[me],
+            src_ref=staged.at[pl.ds(peer_of(step) * 2, 2)],
+            dst_ref=arrived_tails.at[pl.ds(me * 2, 2)],
             send_sem=tail_send_sems.at[step],
             recv_sem=tail_recv_sems.at[step],
             device_id=(peer_of(step), place),
@@ -301,8 +313,8 @@
 
     def row_copy(step):
         return pltpu.make_async_remote_copy(
-            src_ref=staged_rows.at[peer_of(step)],
-            dst_ref=arrived_rows.at[me],
+            src_ref=staged_rows.at[pl.ds(peer_of(step) * 2, 2)],
+            dst_ref=arrived_rows.at[pl.ds(me * 2, 2)],
             send_sem=row_send_sems.at[step],
             recv_sem=row_recv_sems.at[step],
             device_id=(peer_of(step), place),
@@ -345,9 +357,6 @@
     lax.fori_loop(0, branches_here, widen, 0)
     spread(branch_length_ref, length_ref)
     spread(branch_prompt_ref, second_ref, me * cache.shape[0])
-    store_slots = pltpu.make_async_copy(slot_table, slots_out, load_sems.at[0])
-    store_slots.start()
-    store_slots.wait()
     load_query.wait()
     load_residual.wait()
     load_cache.wait()
@@ -385,7 +394,7 @@
             rows = summed[i * spans : (i + 1) * spans]
             rows += residual_ref[i, pl.ds(first, spans)].astype(jnp.float32)
             keep = jnp.concatenate([keep_rows[pl.ds(first, spans)]] * (width // HEAD), axis=1) > 0
-            rows_out[i, pl.ds(first, spans)] = jnp.where(keep, rows, 0.0).astype(rows_out.dtype)
+            mixed_out[i, pl.ds(first, spans)] = jnp.where(keep, rows, 0.0).astype(mixed_out.dtype)
             for at in range(0, width, HEAD):
                 wide_rows[pl.ds(first, spans), i * (width // HEAD) + at // HEAD] = rows[
                     :, at : at + HEAD
@@ -417,7 +426,7 @@
         for kind in range(2):
             rows = written_rows(tails[branch, kind], fresh_of(fresh_ref, branch, kind), length)
             rows = jnp.where(keep, rows.astype(jnp.float32), 0.0)
-            tails[branch, kind] = rows.astype(tails.dtype)
+            tails_out[branch, kind] = rows.astype(tails_out.dtype)
         return carry
 
     def finish_chunk(chunk, carry):
@@ -427,13 +436,13 @@
     wide_rows[...] = jnp.zeros_like(wide_rows)
     lax.fori_loop(0, chunks, finish_chunk, 0)
 
-    def pack_rows(slot, carry):
-        staged_rows[slot // 2, slot % 2] = wide_rows[
-            slot_scalars[slot // 2, slot % 2]
-        ].astype(staged_rows.dtype)
-        return carry
-
-    lax.fori_loop(0, groups * 2, pack_rows, 0)
+    def pack_rows(group, carry):
+        for pick in range(2):
+            rows = wide_rows[slot_scalars[group, pick]]
+            staged_rows[group * 2 + pick] = rows.astype(staged_rows.dtype)
+        return carry
+
+    lax.fori_loop(0, groups, pack_rows, 0)
 
     def send_rows(step, carry):
         row_copy(step).start()
@@ -441,16 +450,52 @@
 
     lax.fori_loop(1, groups, send_rows, 0)
     lax.fori_loop(0, branches_here, settle, 0)
-    store_home = pltpu.make_async_copy(tails, home_out, load_sems.at[1])
-    store_home.start()
-    store_home.wait()
-
-    def drain(step, carry):
-        row_copy(step).wait()
-        tail_copy(step).wait()
-        return carry
-
-    lax.fori_loop(1, groups, drain, 0)
+    for pick in range(2):
+        arrived_tails[me * 2 + pick] = jnp.zeros(arrived_tails.shape[1:], arrived_tails.dtype)
+        arrived_rows[me * 2 + pick] = jnp.zeros(arrived_rows.shape[1:], arrived_rows.dtype)
+
+    def drain_sent(step, carry):
+        tail_copy(step).wait_send()
+        row_copy(step).wait_send()
+        return carry
+
+    def drain_rows(step, carry):
+        row_copy(step).wait_recv()
+        return carry
+
+    def drain_tails(step, carry):
+        tail_copy(step).wait_recv()
+        return carry
+
+    def place_row(row, carry):
+        slot = slot_scalars[row, 2]
+        value = arrived_rows[jnp.maximum(slot, 0)].astype(jnp.float32)
+        value = jnp.where(slot >= 0, value, 0.0)
+        for line in range(stage.shape[0]):
+            stage[line, pl.ds(row, 1)] = value[line : line + 1]
+        return carry
+
+    def place_tail(row, carry):
+        slot = slot_scalars[row, 2]
+        at = jnp.maximum(slot, 0)
+        for kind in range(2):
+            value = arrived_tails[at, kind]
+            value = jnp.where(slot >= 0, value, jnp.zeros_like(value))
+            tails_out[branches_here + row, kind] = value
+        return carry
+
+    incoming = groups - 1
+    lax.fori_loop(1, groups, drain_rows, 0)
+    lax.fori_loop(0, incoming, place_row, 0)
+    for i in range(new_count):
+        for at in range(0, width, HEAD):
+            line = i * (width // HEAD) + at // HEAD
+            mixed_out[i, branches_here:, at : at + HEAD] = stage[line, :incoming].astype(
+                mixed_out.dtype
+            )
+    lax.fori_loop(1, groups, drain_sent, 0)
+    lax.fori_loop(1, groups, drain_tails, 0)
+    lax.fori_loop(0, incoming, place_tail, 0)
 
 
 def block(*arrays):
@@ -459,6 +504,7 @@
     new_count, branches_here, width = queries.shape
     spans = GROUP * TILES
     chunks = branches_here // spans
+    slots = branches_here + groups - 1
     rows = new_count * (width // HEAD) * GROUP
     kind = queries.dtype
     vmem = pl.BlockSpec(memory_space=pltpu.VMEM)
@@ -472,15 +518,15 @@
     return pl.pallas_call(
         body,
         out_shape=[
-            pltpu.VMEM(queries.shape, kind),
-            pltpu.VMEM((groups, 2, ROW, HEAD), kind),
-            pltpu.VMEM((groups, 2) + tails.shape[1:], kind),
-            pltpu.VMEM(tails.shape, kind),
-            pltpu.VMEM((groups, HEAD), jnp.int32),
+            pltpu.VMEM((new_count, slots, width), kind),
+            pltpu.VMEM((slots,) + tails.shape[1:], kind),
         ],
         in_specs=[pl.BlockSpec(memory_space=pltpu.HBM)] * 9,
-        out_specs=[vmem, hbm, hbm, hbm, hbm],
+        out_specs=[vmem, vmem],
         scratch_shapes=[
+            pltpu.VMEM((groups * 2, ROW, HEAD), kind),
+            pltpu.VMEM((groups * 2,) + tails.shape[1:], kind),
+            pltpu.VMEM((new_count * (width // HEAD), groups, HEAD), jnp.float32),
             pltpu.SMEM(lengths.shape, jnp.int32),
             pltpu.SMEM(prompt_of.shape, jnp.int32),
             pltpu.VMEM(moves.shape, jnp.int32),
@@ -495,8 +541,8 @@
             pltpu.VMEM(tails.shape, kind),
             pltpu.VMEM(cache.shape, kind),
             pltpu.VMEM(proj.shape, kind),
-            pltpu.VMEM((groups, 2) + tails.shape[1:], kind),
-            pltpu.VMEM((groups, 2, ROW, HEAD), kind),
+            pltpu.VMEM((groups * 2,) + tails.shape[1:], kind),
+            pltpu.VMEM((groups * 2, ROW, HEAD), kind),
             pltpu.VMEM((2, new_count, branches_here, HEAD), jnp.float32),
             pltpu.VMEM((rows, cache.shape[2]), jnp.float32),
             pltpu.VMEM(queries.shape, kind),
@@ -525,116 +571,33 @@
     )(*(pltpu.with_memory_space_constraint(array, pltpu.HBM) for array in arrays))
 
 
-def place_kernel(
-    slots_ref,
-    rows_in,
-    arrived_rows_in,
-    home_in,
-    arrived_in,
-    mixed_ref,
-    out_ref,
-    rows,
-    arrived_rows,
-    blank,
-    stage,
-    sems,
-    load_sems,
-):
-    incoming = sems.shape[0]
-    new_count, first, width = rows.shape
-    lines = new_count * (width // HEAD)
-    parts = load_sems.shape[0] - 2
-    share = first // parts
-    load_rows = pltpu.make_async_copy(rows_in, rows, load_sems.at[0])
-    load_arrived = pltpu.make_async_copy(arrived_rows_in, arrived_rows, load_sems.at[1])
-
-    def home_copy(part):
-        at = pl.ds(part * share, share)
-        return pltpu.make_async_copy(home_in.at[at], out_ref.at[at], load_sems.at[2 + part])
-
-    def row_copy(source, row):
-        return pltpu.make_async_copy(source, out_ref.at[first + row], sems.at[row])
-
-    load_arrived.start()
-    load_rows.start()
-    for part in range(parts):
-        home_copy(part).start()
-    blank[...] = jnp.zeros_like(blank)
-    stage[...] = jnp.zeros_like(stage)
-    count = slots_ref[0, 4]
-
-    def start(slot, carry):
-        row = slots_ref[slot // 2, 2 + slot % 2]
-
-        @pl.when(row >= 0)
-        def _():
-            row_copy(arrived_in.at[slot], row).start()
-
-        return carry
-
-    def clear(row, carry):
-        row_copy(blank, row).start()
-        return carry
-
-    def stage_row(slot, carry):
-        row = slots_ref[slot // 2, 2 + slot % 2]
-
-        @pl.when(row >= 0)
-        def _():
-            value = arrived_rows[slot].astype(jnp.float32)
-            for line in range(lines):
-                stage[line, pl.ds(row, 1)] = value[line : line + 1]
-
-        return carry
-
-    def done(row, carry):
-        row_copy(blank, row).wait()
-        return carry
-
-    lax.fori_loop(0, arrived_in.shape[0], start, 0)
-    lax.fori_loop(count, incoming, clear, 0)
-    load_arrived.wait()
-    lax.fori_loop(0, arrived_in.shape[0], stage_row, 0)
-    load_rows.wait()
-    for i in range(new_count):
-        mixed_ref[i, :first] = rows[i]
-        for at in range(0, width, HEAD):
-            line = i * (width // HEAD) + at // HEAD
-            mixed_ref[i, first:, at : at + HEAD] = stage[line, :incoming].astype(mixed_ref.dtype)
-    lax.fori_loop(0, incoming, done, 0)
-    for part in range(parts):
-        home_copy(part).wait()
-
-
-def place(slot_table, rows, arrived_rows, home, arrived, incoming):
-    new_count, branches_here, width = rows.shape
-    slots = branches_here + incoming
-    smem = pl.BlockSpec(memory_space=pltpu.SMEM)
-    vmem = pl.BlockSpec(memory_space=pltpu.VMEM)
+def store_kernel(mixed_in, tails_in, mixed_ref, tails_ref, sems):
+    rows = tails_in.shape[0]
+    share = -(-rows // PARTS)
+    copies = [pltpu.make_async_copy(mixed_in, mixed_ref, sems.at[PARTS])]
+    for part in range(PARTS):
+        at = pl.ds(part * share, min(share, rows - part * share))
+        copies.append(pltpu.make_async_copy(tails_in.at[at], tails_ref.at[at], sems.at[part]))
+    for copy in copies:
+        copy.start()
+    for copy in copies:
+        copy.wait()
+
+
+def store(mixed, tails):
     hbm = pl.BlockSpec(memory_space=pl.ANY)
     return pl.pallas_call(
-        place_kernel,
-        out_shape=[
-            jax.ShapeDtypeStruct((new_count, slots, width), rows.dtype),
-            jax.ShapeDtypeStruct((slots,) + home.shape[1:], home.dtype),
-        ],
-        in_specs=[smem] + [hbm] * 4,
-        out_specs=[vmem, hbm],
-        scratch_shapes=[
-            pltpu.VMEM(rows.shape, rows.dtype),
-            pltpu.VMEM(arrived_rows.shape, rows.dtype),
-            pltpu.VMEM(home.shape[1:], home.dtype),
-            pltpu.VMEM((new_count * (width // HEAD), incoming + 1, HEAD), jnp.float32),
-            pltpu.SemaphoreType.DMA((incoming,)),
-            pltpu.SemaphoreType.DMA((2 + HOME_PARTS,)),
-        ],
+        store_kernel,
+        out_shape=[jax.ShapeDtypeStruct(array.shape, array.dtype) for array in (mixed, tails)],
+        in_specs=[hbm] * 2,
+        out_specs=[hbm] * 2,
+        scratch_shapes=[pltpu.SemaphoreType.DMA((PARTS + 1,))],
         compiler_params=pltpu.CompilerParams(vmem_limit_bytes=8 * MIB),
-    )(slot_table, rows, arrived_rows, home, arrived)
+    )(mixed, tails)
 
 
 def on_device(queries, prompt_cache, tails, fresh, residual, out_proj, lengths, prompt_of, moves):
-    groups = lax.axis_size("dp")
-    rows, arrived_rows, arrived_tails, home, slot_table = block(
+    mixed, tails_out = block(
         lengths,
         prompt_of,
         jnp.transpose(moves),
@@ -645,14 +608,7 @@
         prompt_cache,
         out_proj,
     )
-    mixed, tails_out = place(
-        slot_table,
-        rows,
-        arrived_rows.reshape((groups * 2,) + arrived_rows.shape[2:]),
-        home,
-        arrived_tails.reshape((groups * 2,) + arrived_tails.shape[2:]),
-        groups - 1,
-    )
+    mixed, tails_out = store(mixed, tails_out)
     return (jnp.transpose(mixed, (1, 0, 2)), tails_out)
 
 

time: 70 us -> 68.6 us (0.980)
  Pallas kernels: 69.2 us -> 67.7 us
    pallas_call x2, Pallas kernels: 69.2 us -> 67.7 us  [the longest x1 65.6 us: block(): pl.pallas_call(body, out_shape=[pltpu.VMEM((new_count, slots, width), kin...]
where the time goes in v3:
time: 68.6 us; the launch traced here: 68.4 us
  Pallas kernels  67.7 us (99%)
    pallas_call x1, Pallas kernels, block(): pl.pallas_call(body, out_shape=[pltpu.VMEM((new_count, slots, width), kin...  65.6 us
    pallas_call x1, Pallas kernels, store(): pl.pallas_call(store_kernel, out_shape=[jax.ShapeDtypeStruct(array.shape,...  2.16 us

profile of v3, /device:TPU:16, one launch (start us, length us, event | category | flops | bytes accessed | tf_op | source)
XLA Modules:
  0.0 68.4 jit_solution(10521764014224695863)
XLA Ops:
  0.6 65.6 %shard_map.104 = (bf16[3,127,512]{2,1,0:T(8,128)(2,1)S(1)}, bf16[127,2,64,128]{3,2,1,0:T(8,128)(2,1)S(1)}) custom-call(s32[96]{0:T(128)} %refs_0_.1, s32[96]{0:T(128)} %refs_1_.1, s32[3,496]{1,0:T(4,128)} %bitcast.7, bf16[3,96,512]{2,1,0:T(8,128)(2,1)} %bitcast.5, bf16[3,96,512]{2,1,0:T(8,128)(2,1)} %bitcast.6, bf16[96,3,2,128]{3,2,1,0:T(2,128)(2,1)} %refs_5_.1, ...), custom_call_target="tpu_custom_call" | custom-call | flops 4831838208 | bytes 20971520 | tf_op jit(solution)/shard_map/pallas_call | solution.py:518
  66.2 2.2 %shard_map.105 = (bf16[3,127,512]{2,1,0:T(8,128)(2,1)}, bf16[127,2,64,128]{3,2,1,0:T(8,128)(2,1)}) custom-call(bf16[3,127,512]{2,1,0:T(8,128)(2,1)S(1)} %get-tuple-element.6.mixed_in, bf16[127,2,64,128]{3,2,1,0:T(8,128)(2,1)S(1)} %get-tuple-element.7.tails_in), custom_call_target="tpu_custom_call" | custom-call | tf_op jit(solution)/shard_map/pallas_call | solution.py:589

commit v4 on v3

--- a/solution.py
+++ b/solution.py
@@ -127,7 +127,7 @@
             heads[i, pl.ds(first, GROUP), h * HEAD : (h + 1) * HEAD] = result[at : at + GROUP]
 
 
-def find_slots(me, groups, branches_here, moves, slot_table, keep_rows):
+def find_departures(me, groups, branches_here, moves, slot_table):
     branch, source, target = (moves[at : at + 1] for at in range(3))
     entries = moves.shape[1]
     group = lax.broadcasted_iota(jnp.int32, (groups, entries), 0)
@@ -137,7 +137,17 @@
     code = jnp.where((source == me) & (target == group), entry * HEAD + local, -1)
     last = jnp.max(code, axis=1, keepdims=True)
     first = jnp.min(jnp.where(code >= 0, code, far), axis=1, keepdims=True)
-    sent = [jnp.where(first < far, first % HEAD, 0), jnp.where(last >= 0, last % HEAD, 0)]
+    first = jnp.where(first < far, first % HEAD, 0)
+    last = jnp.where(last >= 0, last % HEAD, 0)
+    column = lax.broadcasted_iota(jnp.int32, slot_table.shape, 1)
+    slot_table[...] = jnp.where(column == 0, first, last)
+
+
+def find_arrivals(me, groups, branches_here, moves, slot_table, keep_rows):
+    branch, source, target = (moves[at : at + 1] for at in range(3))
+    entries = moves.shape[1]
+    group = lax.broadcasted_iota(jnp.int32, (groups, entries), 0)
+    entry = lax.broadcasted_iota(jnp.int32, (groups, entries), 1)
     here = target == me
     code = jnp.where(here & (source == group), entry, -1)
     last = jnp.max(code, axis=1, keepdims=True)
@@ -156,14 +166,11 @@
     once = flat(jnp.where(last >= 0, arrival(first), -1))
     twice = flat(jnp.where(last > first, arrival(last), -1))
     slot = jnp.where(once == row, column * 2, jnp.where(twice == row, column * 2 + 1, -1))
-    sent.append(jnp.max(slot, axis=1, keepdims=True))
+    slot = jnp.max(slot, axis=1, keepdims=True)
     column = lax.broadcasted_iota(jnp.int32, slot_table.shape, 1)
-    table = jnp.zeros(slot_table.shape, jnp.int32)
-    for at, value in enumerate(sent):
-        table = jnp.where(column == at, value, table)
-    slot_table[...] = table
+    slot_table[...] = jnp.where(column == 2, slot, slot_table[...])
     row = lax.broadcasted_iota(jnp.int32, (branches_here, entries), 0)
-    gone = jnp.where((source == me) & (local == row), 1, 0)
+    gone = jnp.where((source == me) & (branch - me * branches_here == row), 1, 0)
     gone = jnp.max(gone, axis=1, keepdims=True)
     keep_rows[...] = jnp.broadcast_to(1 - gone, keep_rows.shape)
 
@@ -279,7 +286,7 @@
     load_cache.start()
     load_proj.start()
     load_moves.wait()
-    find_slots(me, groups, branches_here, moves, slot_table, keep_rows)
+    find_departures(me, groups, branches_here, moves, slot_table)
     load_slots = pltpu.make_async_copy(slot_table, slot_scalars, load_sems.at[7])
     load_slots.start()
     load_slots.wait()
@@ -288,7 +295,8 @@
     load_lengths.wait()
     load_prompts.wait()
 
-    def pack(group, carry):
+    def pack(step, carry):
+        group = peer_of(step)
         for pick in range(2):
             branch = slot_scalars[group, pick]
             length = branch_length_ref[branch]
@@ -296,9 +304,9 @@
                 staged[group * 2 + pick, kind] = written_rows(
                     tails[branch, kind], fresh_of(fresh_ref, branch, kind), length
                 )
-        return carry
-
-    lax.fori_loop(0, groups, pack, 0)
+        tail_copy(step).start()
+        return carry
+
     pl.semaphore_wait(barrier, groups - 1 + 1 + chips - 1)
 
     def tail_copy(step):
@@ -341,11 +349,10 @@
             device_id_type=MESH,
         )
 
-    def send_tails(step, carry):
-        tail_copy(step).start()
-        return carry
-
-    lax.fori_loop(1, groups, send_tails, 0)
+    lax.fori_loop(1, groups, pack, 0)
+    find_arrivals(me, groups, branches_here, moves, slot_table, keep_rows)
+    load_slots.start()
+    load_slots.wait()
 
     def widen(branch, carry):
         for i in range(new_count):
@@ -485,6 +492,8 @@
         return carry
 
     incoming = groups - 1
+    lax.fori_loop(1, groups, drain_tails, 0)
+    lax.fori_loop(0, incoming, place_tail, 0)
     lax.fori_loop(1, groups, drain_rows, 0)
     lax.fori_loop(0, incoming, place_row, 0)
     for i in range(new_count):
@@ -494,8 +503,6 @@
                 mixed_out.dtype
             )
     lax.fori_loop(1, groups, drain_sent, 0)
-    lax.fori_loop(1, groups, drain_tails, 0)
-    lax.fori_loop(0, incoming, place_tail, 0)
 
 
 def block(*arrays):

time: 68.6 us -> 67.9 us (0.990)
  no operation moved by 1% of the time
where the time goes in v4:
time: 67.9 us; the launch traced here: 67.8 us
  Pallas kernels  67.1 us (99%)
    pallas_call x1, Pallas kernels, block(): pl.pallas_call(body, out_shape=[pltpu.VMEM((new_count, slots, width), kin...  65 us
    pallas_call x1, Pallas kernels, store(): pl.pallas_call(store_kernel, out_shape=[jax.ShapeDtypeStruct(array.shape,...  2.16 us

profile of v4, /device:TPU:16, one launch (start us, length us, event | category | flops | bytes accessed | tf_op | source)
XLA Modules:
  0.0 67.8 jit_solution(5847260976199524018)
XLA Ops:
  0.6 65.0 %shard_map.104 = (bf16[3,127,512]{2,1,0:T(8,128)(2,1)S(1)}, bf16[127,2,64,128]{3,2,1,0:T(8,128)(2,1)S(1)}) custom-call(s32[96]{0:T(128)} %refs_0_.1, s32[96]{0:T(128)} %refs_1_.1, s32[3,496]{1,0:T(4,128)} %bitcast.7, bf16[3,96,512]{2,1,0:T(8,128)(2,1)} %bitcast.5, bf16[3,96,512]{2,1,0:T(8,128)(2,1)} %bitcast.6, bf16[96,3,2,128]{3,2,1,0:T(2,128)(2,1)} %refs_5_.1, ...), custom_call_target="tpu_custom_call" | custom-call | flops 4831838208 | bytes 20971520 | tf_op jit(solution)/shard_map/pallas_call | solution.py:525
  65.6 2.2 %shard_map.105 = (bf16[3,127,512]{2,1,0:T(8,128)(2,1)}, bf16[127,2,64,128]{3,2,1,0:T(8,128)(2,1)}) custom-call(bf16[3,127,512]{2,1,0:T(8,128)(2,1)S(1)} %get-tuple-element.6.mixed_in, bf16[127,2,64,128]{3,2,1,0:T(8,128)(2,1)S(1)} %get-tuple-element.7.tails_in), custom_call_target="tpu_custom_call" | custom-call | tf_op jit(solution)/shard_map/pallas_call | solution.py:596
